TPU v7x, 32 devices: a whole 2x2x4 slice. The times are simulated.
32 devices in a mesh: dp: 4 (over y, x), fsdp: 8 (over z, core).
Axes of the slice: x: 2, y: 2, z: 4, core: 2. Of those that a mesh axis runs over, the one named last changes fastest.
Arguments:
- tokens: bfloat16 [64, 197, 768], P(('dp', 'fsdp')), may hold values from -6 to 6
- counts: int32 [64], P(('dp', 'fsdp')), may hold values from 65 to 197, as said below
- params_first: bfloat16 [7098368], P(('dp', 'fsdp')), may hold values from -3 to 3
- params_second: bfloat16 [7098368], P(('dp', 'fsdp')), may hold values from -3 to 3
- cotangent: bfloat16 [64, 197, 768], P(('dp', 'fsdp')), may hold values from -6 to 6
Outputs:
- output: bfloat16 [64, 197, 768], P(('dp', 'fsdp'))
- grad_tokens: bfloat16 [64, 197, 768], P(('dp', 'fsdp'))
- grad_first: float32 [7098368], P(('dp', 'fsdp'))
- grad_second: float32 [7098368], P(('dp', 'fsdp'))
Inputs may be any that keep to these rules, and one draw needn't show every extreme that they name: Keys 0 to counts - 1 of an image are valid; some image has all 197.
All inputs are finite; a program needn't handle non-finite values.
Results may differ from a plain program's by a relative error of at most 0.015.
Values may be sent and summed in bfloat16 or wider, within the bound.
No kernel may reach another device: no remote copies, remote signals or barrier semaphores. Data moves between devices by JAX's collectives and lax.ppermute only.
A program may use at most 256 MiB of HBM per device.

v0:
```python
import functools
import math

import jax
import jax.numpy as jnp
import numpy as np
from jax import lax
from jax.experimental import pallas as pl
from jax.experimental.pallas import tpu as pltpu
from jax.sharding import PartitionSpec as P

D = 768
HEADS = 12
HEAD = D // HEADS
FF = 3072
GRID = 14
SEQ = 197
RELS = 732
ROWS = 208
LANES = 128
TILE = 16
AXES = ("dp", "fsdp")
VMEM_LIMIT = 56 * 2**20

EPSILON = 1e-06
NEGATIVE = -1000000000.0

ENTRIES = [
    ("norm1_gain", (D,)),
    ("norm1_bias", (D,)),
    ("qkv_weight", (D, 3 * D)),
    ("query_bias", (D,)),
    ("value_bias", (D,)),
    ("relative_table", (RELS, HEADS)),
    ("proj_weight", (D, D)),
    ("proj_bias", (D,)),
    ("gamma_attn", (D,)),
    ("norm2_gain", (D,)),
    ("norm2_bias", (D,)),
    ("fc1_weight", (D, FF)),
    ("fc1_bias", (FF,)),
    ("fc2_weight", (FF, D)),
    ("fc2_bias", (D,)),
    ("gamma_mlp", (D,)),
]
WEIGHTS = {name: dims for name, dims in ENTRIES if name.endswith("weight")}
SIZES = dict(ENTRIES)
VECTORS = [
    "norm1_gain",
    "norm1_bias",
    "query_bias",
    "value_bias",
    "proj_bias",
    "gamma_attn",
    "norm2_gain",
    "norm2_bias",
    "fc2_bias",
    "gamma_mlp",
]
ROW = {name: i for i, name in enumerate(VECTORS)}


def count_rows(dims):
    return -(-math.prod(dims) // LANES)


def virtual_starts():
    starts, at = {}, 0
    for name, dims in ENTRIES:
        starts[name] = at
        at += count_rows(dims)
    return starts, at


STARTS, VIRTUAL = virtual_starts()
SHIFT = RELS * HEADS % LANES
TABLE_END = STARTS["proj_weight"]


def tile_order():
    parts = []
    for name, (depth, width) in WEIGHTS.items():
        across = width // LANES
        rows = STARTS[name] + np.arange(depth * across).reshape(depth // TILE, TILE, across)
        parts.append(rows.transpose(0, 2, 1).reshape(-1))
    return np.concatenate(parts)


def small_order():
    groups = [VECTORS, ["fc1_bias"], ["relative_table"]]
    rows = []
    for group in groups:
        for name in group:
            rows += [STARTS[name] + i for i in range(count_rows(SIZES[name]))]
        rows += [-1] * (-len(rows) % 8)
    return np.array(rows)


TILE_ROWS = tile_order()
SMALL_ROWS = small_order()
TILES = len(TILE_ROWS) // TILE


def tie(*trees):
    leaves, structure = jax.tree.flatten(trees)
    tied = iter(lax.optimization_barrier([leaf for leaf in leaves if isinstance(leaf, jax.Array)]))
    return structure.unflatten([next(tied) if isinstance(leaf, jax.Array) else leaf for leaf in leaves])


def halo(block, before, after, devices, join=True):
    rows = block.shape[-2]
    pieces = [block] if join else []
    for hop in range(1, -(-before // rows) + 1):
        take = min(rows, before - (hop - 1) * rows)
        perm = [(i, i + hop) for i in range(devices - hop)]
        pieces.insert(0, lax.ppermute(block[..., rows - take :, :], AXES, perm))
    for hop in range(1, -(-after // rows) + 1):
        take = min(rows, after - (hop - 1) * rows)
        perm = [(i + hop, i) for i in range(devices - hop)]
        pieces.append(lax.ppermute(block[..., :take, :], AXES, perm))
    return jnp.concatenate(pieces, axis=-2)


def pick_rows(index, source):
    chosen = index[:, None] == lax.broadcasted_iota(jnp.int32, (1, source.shape[0]), 1)
    return jnp.dot(chosen.astype(jnp.bfloat16), source.astype(jnp.bfloat16), preferred_element_type=jnp.float32)


def round_up(value, unit):
    return -(-value // unit) * unit


class Owned:
    def __init__(self, flats, me, devices):
        length = flats[0].shape[0] // LANES
        share = len(TILE_ROWS) // devices
        starts = np.arange(devices)[:, None] * length
        wanted = TILE_ROWS.reshape(devices, share) - starts
        before = round_up(max(0, -wanted.min()) + 1, TILE)
        after = round_up(max(0, wanted.max() + 1 - length), TILE)
        smalls = SMALL_ROWS[None] - starts
        smalls = np.where((smalls >= 0) & (smalls < length), smalls + before - 1, -1)
        self.wanted = self.mine(wanted + before - 1, me)
        self.smalls = self.mine(smalls, me)
        around = halo(jnp.stack([flat.reshape(length, LANES) for flat in flats]), before, after, devices)
        shifted = jnp.concatenate([around[:, :-1, SHIFT:], around[:, 1:, :SHIFT]], axis=2)
        at = me * length - before + 1 + lax.broadcasted_iota(jnp.int32, (1, shifted.shape[1], 1), 1)
        self.virtual = jnp.where(at < TABLE_END, around[:, 1:], shifted)

    @staticmethod
    def mine(table, me):
        return lax.dynamic_index_in_dim(jnp.asarray(table.astype(np.int32)), me, 0, keepdims=False)

    def small_rows(self, *after):
        virtual, *_ = tie(self.virtual, *after)
        return jnp.stack([pick_rows(self.smalls, rows).astype(jnp.bfloat16) for rows in virtual])

    def share(self, number, *after):
        rows = self.virtual[number]
        if after:
            rows, *_ = tie(rows, *after)
        return pick_rows(self.wanted, rows).astype(jnp.bfloat16)


class FlatShare:
    def __init__(self, me, devices, flat_length):
        length = flat_length // LANES // devices
        share = len(TILE_ROWS) // devices
        place = np.full(max(VIRTUAL, devices * length + 1), -1, np.int64)
        place[TILE_ROWS] = np.arange(len(TILE_ROWS))
        small_place = np.full(place.shape, -1, np.int64)
        small_place[SMALL_ROWS[SMALL_ROWS >= 0]] = np.flatnonzero(SMALL_ROWS >= 0)
        span = np.arange(devices)[:, None] * length + np.arange(length + 1)[None]
        relative = place[span] - np.arange(devices)[:, None] * share
        has = place[span] >= 0
        self.before = round_up(max(0, -relative[has].min()), TILE)
        self.after = round_up(max(0, relative[has].max() + 1 - share), TILE)
        smalls_at = self.before + share + self.after
        index = np.where(has, relative + self.before, -1)
        index = np.where(small_place[span] >= 0, small_place[span] + smalls_at, index)
        self.index = Owned.mine(index, me)
        self.at = me * length + lax.broadcasted_iota(jnp.int32, (length, 1), 0)
        self.devices = devices

    def __call__(self, owned, smalls):
        owned = owned.astype(jnp.bfloat16)
        share = owned.shape[0]
        around = halo(owned, self.before, self.after, self.devices, join=False)
        ends = self.before + share
        here = jnp.concatenate([owned, smalls.astype(jnp.bfloat16)], axis=0)
        index = self.index - self.before
        outside = (self.index < self.before) | ((self.index >= ends) & (self.index < ends + self.after))
        index = jnp.where(outside, -1, jnp.where(self.index >= ends, index - self.after, index))
        virtual = pick_rows(index, here)
        index = jnp.where(self.index < self.before, self.index, self.index - share)
        index = jnp.where(outside, index, -1)
        virtual = virtual + pick_rows(index, around)
        here, following = virtual[:-1], virtual[1:]
        lane = lax.broadcasted_iota(jnp.int32, (1, LANES), 1)
        shifted = jnp.concatenate([here[:, LANES - SHIFT :], following[:, : LANES - SHIFT]], axis=1)
        straight = (self.at < TABLE_END - 1) | ((self.at == TABLE_END - 1) & (lane < SHIFT))
        return jnp.where(straight, here, shifted).reshape(-1)


VECTOR_ROWS = D // LANES
FC1_AT = round_up(len(VECTORS) * VECTOR_ROWS, 8)
TABLE_AT = FC1_AT + FF // LANES
TABLE_ROWS = count_rows(SIZES["relative_table"])
LATER = 4


def table_entries(rows):
    tables = rows[:, TABLE_AT : TABLE_AT + TABLE_ROWS].reshape(2, -1)[:, : RELS * HEADS].reshape(2, RELS, HEADS)
    return jnp.pad(tables.transpose(0, 2, 1), ((0, 0), (0, 16 - HEADS), (0, ENTRY_LANES - RELS)))


def small_gradients(first, later, tables):
    tables = tables.reshape(2, RELS * HEADS)
    tables = jnp.pad(tables, ((0, 0), (0, round_up(TABLE_ROWS, 8) * LANES - RELS * HEADS))).reshape(2, -1, LANES)
    return jnp.concatenate([jnp.stack(first), jnp.stack(later), tables], axis=1)


SIDE = 2 * GRID - 1
WINDOW = round_up(SIDE * GRID, LANES) + LANES
WIDE = round_up(ROWS, LANES)


ENTRY_LANES = round_up(RELS, LANES)
HEAD_ROWS = 2 * 16


def entry_choice(column, transposed):
    shape = (1, WINDOW) if transposed else (WINDOW, 1)
    source = lax.broadcasted_iota(jnp.int32, shape, 1 if transposed else 0)
    group = source // GRID
    target = (SIDE - 1 - group) * SIDE - (source - group * GRID) + GRID - 1 + column
    target = jnp.where(source < SIDE * GRID, target, -1)
    entries = (ENTRY_LANES, 1) if transposed else (1, ENTRY_LANES)
    entry = lax.broadcasted_iota(jnp.int32, entries, 0 if transposed else 1)
    return (entry == target).astype(jnp.float32).astype(jnp.bfloat16)


def bias_kernel(entries_ref, bias_ref, windows_ref):
    for column in range(GRID):
        windows_ref[column] = product(entries_ref[...], entry_choice(column, True), NN)
    lane = lax.broadcasted_iota(jnp.int32, (1, WIDE), 1)
    inner = (lane >= 1) & (lane < SEQ)

    def head(i, _):
        ends = entries_ref[pl.ds(pl.multiple_of(i // 16 * 16, 16), 16), :].astype(jnp.float32)
        picked = lax.broadcasted_iota(jnp.int32, (16, 1), 0) == i % 16
        ends = jnp.sum(jnp.where(picked, ends, 0.0), axis=0, keepdims=True)
        top, left, corner = [ends[:, RELS - k : RELS - k + 1] for k in (3, 2, 1)]
        bias_ref[i] = jnp.zeros(bias_ref.shape[1:], jnp.float32)
        bias_ref[i, 0:1] = jnp.where(inner, top, jnp.where(lane == 0, corner, 0.0))[:, :ROWS]
        spread = jnp.concatenate([windows_ref[column, pl.ds(i, 1)] for column in range(GRID)], axis=0)
        for row in range(GRID):
            start = (GRID - 1 - row) * GRID
            window = pltpu.roll(spread, (1 - start) % WINDOW, 1)[:, :WIDE]
            window = jnp.where(inner, window, jnp.where(lane == 0, left, 0.0))
            bias_ref[i, 1 + row * GRID : 1 + (row + 1) * GRID] = window[:, :ROWS]
        return 0

    lax.fori_loop(0, HEADS, head, 0)


def bias_of(entries):
    return pl.pallas_call(
        bias_kernel,
        grid=(1,),
        in_specs=[pl.BlockSpec(entries.shape, lambda i: (0, 0))],
        out_specs=pl.BlockSpec((HEADS, ROWS, ROWS), lambda i: (0, 0, 0)),
        out_shape=jax.ShapeDtypeStruct((HEADS, ROWS, ROWS), jnp.float32),
        scratch_shapes=[pltpu.VMEM((GRID, 16, WINDOW), jnp.float32)],
        compiler_params=pltpu.CompilerParams(vmem_limit_bytes=VMEM_LIMIT),
        name="bias",
    )(entries)


def table_kernel(first_ref, second_ref, out_ref, windows_ref, ends_ref):
    lane = lax.broadcasted_iota(jnp.int32, (1, ROWS), 1)
    inner = (lane >= 1) & (lane < SEQ)
    entry = lax.broadcasted_iota(jnp.int32, (1, ENTRY_LANES), 1)
    windows_ref[...] = jnp.zeros_like(windows_ref)
    ends_ref[...] = jnp.zeros_like(ends_ref)
    for number, grad_ref in enumerate((first_ref, second_ref)):

        def head(i, _, number=number, grad_ref=grad_ref):
            total = jnp.zeros((GRID, WINDOW), jnp.float32)
            left = jnp.zeros((1, 1), jnp.float32)
            for row in range(GRID):
                start = (GRID - 1 - row) * GRID
                block = grad_ref[i, 1 + row * GRID : 1 + (row + 1) * GRID]
                left = left + jnp.sum(jnp.where(lane == 0, block, 0.0), keepdims=True)
                block = jnp.where(inner, block, 0.0)
                block = jnp.concatenate([block, jnp.zeros((GRID, WINDOW - ROWS), jnp.float32)], axis=1)
                total = total + pltpu.roll(block, (start - 1) % WINDOW, 1)
            at = pl.ds(number * 16 + i, 1)
            for column in range(GRID):
                windows_ref[column, at] = total[column : column + 1]
            first = grad_ref[i, 0:1]
            top = jnp.sum(jnp.where(inner, first, 0.0), keepdims=True)
            corner = jnp.sum(jnp.where(lane == 0, first, 0.0), keepdims=True)
            ends = jnp.where(entry == RELS - 3, top, jnp.where(entry == RELS - 2, left, 0.0))
            ends_ref[at] = jnp.where(entry == RELS - 1, corner, ends)
            return 0

        lax.fori_loop(0, HEADS, head, 0)
    out_ref[...] = ends_ref[...]
    for column in range(GRID):
        rows = windows_ref[column]
        high = rows.astype(jnp.bfloat16)
        low = (rows - high.astype(jnp.float32)).astype(jnp.bfloat16)
        chosen = entry_choice(column, False)
        out_ref[...] += product(high, chosen, NN) + product(low, chosen, NN)


def tables_from_biases(first, second):
    entries = pl.pallas_call(
        table_kernel,
        grid=(1,),
        in_specs=[pl.BlockSpec(first.shape, lambda i: (0, 0, 0))] * 2,
        out_specs=pl.BlockSpec((HEAD_ROWS, ENTRY_LANES), lambda i: (0, 0)),
        out_shape=jax.ShapeDtypeStruct((HEAD_ROWS, ENTRY_LANES), jnp.float32),
        scratch_shapes=[
            pltpu.VMEM((GRID, HEAD_ROWS, WINDOW), jnp.float32),
            pltpu.VMEM((HEAD_ROWS, ENTRY_LANES), jnp.float32),
        ],
        compiler_params=pltpu.CompilerParams(vmem_limit_bytes=VMEM_LIMIT),
        name="table_back",
    )(first, second)
    return entries.reshape(2, 16, ENTRY_LANES)[:, :HEADS, :RELS].transpose(0, 2, 1)


NT = (((1,), (1,)), ((), ()))
NN = (((1,), (0,)), ((), ()))
TN = (((0,), (0,)), ((), ()))


def product(left, right, dims):
    return lax.dot_general(left, right, dims, preferred_element_type=jnp.float32)


def own_lanes(head):
    lane = lax.broadcasted_iota(jnp.int32, (1, LANES), 1)
    return lane < HEAD if head == 0 else lane >= HEAD


def head_weights(query, key, bias, count, head):
    chosen = jnp.where(own_lanes(head), query, jnp.zeros_like(query))
    scores = product(chosen, key, NT) + bias
    column = lax.broadcasted_iota(jnp.int32, (1, ROWS), 1)
    scores = jnp.where(column < count, scores, NEGATIVE)
    grown = jnp.exp(scores - jnp.max(scores, axis=1, keepdims=True))
    return grown * (1.0 / jnp.sum(grown, axis=1, keepdims=True))


def attention_kernel(pairs, counts_ref, query_ref, key_ref, value_ref, bias_ref, out_ref, weights_ref):
    count = counts_ref[pl.program_id(1)]
    for pair in range(pairs):
        lanes = slice(pair * LANES, (pair + 1) * LANES)
        query, key, value = query_ref[:, lanes], key_ref[:, lanes], value_ref[:, lanes]
        parts = []
        for head in range(2):
            weights = head_weights(query, key, bias_ref[2 * pair + head], count, head).astype(jnp.bfloat16)
            weights_ref[0, 2 * pair + head] = weights
            parts.append(product(weights, value, NN))
        out_ref[:, lanes] = jnp.where(own_lanes(0), parts[0], parts[1]).astype(jnp.bfloat16)


def attention_back_kernel(pairs, query_ref, key_ref, value_ref, grad_ref, weights_ref, out_ref, db_ref):
    image = pl.program_id(1)

    @pl.when(image == 0)
    def _():
        db_ref[...] = jnp.zeros_like(db_ref)

    for pair in range(pairs):
        lanes = slice(pair * LANES, (pair + 1) * LANES)
        query, key, value, grad = query_ref[:, lanes], key_ref[:, lanes], value_ref[:, lanes], grad_ref[:, lanes]
        dq, dk, dv = [], [], []
        for head in range(2):
            low_weights = weights_ref[0, 2 * pair + head]
            weights = low_weights.astype(jnp.float32)
            chosen = jnp.where(own_lanes(head), grad, jnp.zeros_like(grad))
            weighted = weights * product(chosen, value, NT)
            dv.append(product(low_weights, grad, TN))
            grad_scores = weighted - weights * jnp.sum(weighted, axis=1, keepdims=True)
            low = grad_scores.astype(jnp.bfloat16)
            dq.append(product(low, key, NN))
            dk.append(product(low, query, TN))
            db_ref[2 * pair + head] += grad_scores
        first = own_lanes(0)
        out_ref[0, :, lanes] = (jnp.where(first, dq[0], dq[1]) * HEAD**-0.5).astype(jnp.bfloat16)
        out_ref[1, :, lanes] = jnp.where(first, dk[0], dk[1]).astype(jnp.bfloat16)
        out_ref[2, :, lanes] = jnp.where(first, dv[0], dv[1]).astype(jnp.bfloat16)


def attention_specs(pairs):
    steps = D // LANES // pairs
    lanes = [
        pl.BlockSpec((ROWS, pairs * LANES), lambda step, image, *_, part=part: (image, part * steps + step))
        for part in range(3)
    ]
    bias = pl.BlockSpec((2 * pairs, ROWS, ROWS), lambda step, image, *_: (step, 0, 0))
    weights = pl.BlockSpec((1, 2 * pairs, ROWS, ROWS), lambda step, image, *_: (image, step, 0, 0))
    return steps, lanes, bias, weights


def attention(counts, qkv, bias, pairs=6):
    images = qkv.shape[0] // ROWS
    steps, lanes, bias_spec, weights_spec = attention_specs(pairs)
    return pl.pallas_call(
        functools.partial(attention_kernel, pairs),
        grid_spec=pltpu.PrefetchScalarGridSpec(
            num_scalar_prefetch=1,
            grid=(steps, images),
            in_specs=lanes + [bias_spec],
            out_specs=[lanes[0], weights_spec],
        ),
        out_shape=[
            jax.ShapeDtypeStruct((qkv.shape[0], D), jnp.bfloat16),
            jax.ShapeDtypeStruct((images, HEADS, ROWS, ROWS), jnp.bfloat16),
        ],
        compiler_params=pltpu.CompilerParams(vmem_limit_bytes=VMEM_LIMIT),
        name="attention",
    )(counts, qkv, qkv, qkv, bias)


def attention_back(qkv, grad, weights, pairs=3):
    images = qkv.shape[0] // ROWS
    steps, lanes, bias_spec, weights_spec = attention_specs(pairs)
    return pl.pallas_call(
        functools.partial(attention_back_kernel, pairs),
        grid=(steps, images),
        in_specs=lanes + [lanes[0], weights_spec],
        out_specs=[
            pl.BlockSpec((3, ROWS, pairs * LANES), lambda step, image: (0, image, step)),
            bias_spec,
        ],
        out_shape=[
            jax.ShapeDtypeStruct((3, qkv.shape[0], D), jnp.bfloat16),
            jax.ShapeDtypeStruct((HEADS, ROWS, ROWS), jnp.float32),
        ],
        compiler_params=pltpu.CompilerParams(vmem_limit_bytes=VMEM_LIMIT),
        name="attention_back",
    )(qkv, qkv, qkv, grad, weights)


def tile_starts():
    starts, at = {}, 0
    for name, (depth, width) in WEIGHTS.items():
        starts[name] = at
        at += depth // TILE * (width // LANES)
    return starts


FIRST = tile_starts()
MLP_FIRST = FIRST["proj_weight"]
SPAN = 1024


def load_weight(ref, base, name, row, rows, column, columns):
    first, across = FIRST[name] - base, WEIGHTS[name][1] // LANES
    lines = []
    for i in range(rows):
        at = first + (row + i) * across + column
        lines.append(jnp.concatenate([ref[at + j] for j in range(columns)], axis=1))
    return jnp.concatenate(lines, axis=0)


def gelu_and_slope(values):
    size = jnp.abs(values)
    step = 1.0 / (1.0 + (0.3275911 / math.sqrt(2.0)) * size)
    bell = jnp.exp(-0.5 * values * values)
    series = 1.061405429
    for term in (-1.453152027, 1.421413741, -0.284496736, 0.254829592):
        series = series * step + term
    tail = 0.5 * series * step * bell
    area = jnp.where(values < 0, tail, 1.0 - tail)
    return values * area, area + values * bell * (1.0 / math.sqrt(2.0 * math.pi))


def norm_parts(values):
    centre = values - jnp.mean(values, axis=-1, keepdims=True)
    spread = jnp.mean(centre * centre, axis=-1, keepdims=True)
    inverse = lax.rsqrt(spread + EPSILON)
    return centre * inverse, inverse


def norm_back(grad, normal, inverse, gain):
    scaled = grad * gain
    first = jnp.mean(scaled, axis=-1, keepdims=True)
    second = jnp.mean(scaled * normal, axis=-1, keepdims=True)
    return (scaled - first - normal * second) * inverse


def wide_row(ref, first, count):
    return jnp.concatenate([ref[first + i : first + i + 1] for i in range(count)], axis=1)


def vector(ref, name):
    return wide_row(ref, ROW[name] * VECTOR_ROWS, VECTOR_ROWS)


def put_vector(ref, row, values):
    sums = jnp.sum(values, axis=0, keepdims=True)
    for i in range(sums.shape[1] // LANES):
        ref[row + i : row + i + 1] = sums[:, i * LANES : (i + 1) * LANES]


def later_row(name):
    return (ROW[name] - LATER) * VECTOR_ROWS


def whole_spec(shape):
    return pl.BlockSpec(shape, lambda *_: (0,) * len(shape))


ANYWHERE = pl.BlockSpec(memory_space=pl.ANY)
PARAMS = pltpu.CompilerParams(vmem_limit_bytes=VMEM_LIMIT)


def low_like(*shape):
    return jax.ShapeDtypeStruct(shape, jnp.bfloat16)


def full_like(*shape):
    return jax.ShapeDtypeStruct(shape, jnp.float32)


def project_kernel(places, slots, at_ref, *refs):
    parts, refs = refs[: len(slots)], refs[len(slots) :]
    hidden_ref, vectors_ref, normed_ref, qkv_ref, tiles_ref, whole_ref, sems, out_sem = refs
    copies = copies_in(places, at_ref, parts, slots, whole_ref, sems)
    for copy in copies:
        copy.start()
    normal, _ = norm_parts(hidden_ref[...])
    normed_ref[...] = (normal * vector(vectors_ref, "norm1_gain") + vector(vectors_ref, "norm1_bias")).astype(
        jnp.bfloat16
    )
    for copy in copies:
        copy.wait()
    leaving = pltpu.make_async_copy(whole_ref, tiles_ref, out_sem)
    leaving.start()
    across = D // LANES
    for part in range(3):
        weight = load_weight(whole_ref, 0, "qkv_weight", 0, D // TILE, part * across, across)
        rows = product(normed_ref[...], weight, NN)
        if part == 0:
            rows = (rows + vector(vectors_ref, "query_bias")) * HEAD**-0.5
        if part == 2:
            rows = rows + vector(vectors_ref, "value_bias")
        qkv_ref[:, part * D : (part + 1) * D] = rows.astype(jnp.bfloat16)
    leaving.wait()


def project(places, position, parts, hidden, vectors):
    arrays = [array for array, _ in parts]
    slots = [listed for _, listed in parts]
    rows = hidden.shape[0]
    return pl.pallas_call(
        functools.partial(project_kernel, places, slots),
        grid_spec=pltpu.PrefetchScalarGridSpec(
            num_scalar_prefetch=1,
            grid=(1,),
            in_specs=[ANYWHERE] * len(arrays) + [whole_spec((rows, D)), whole_spec(vectors.shape)],
            out_specs=[whole_spec((rows, D)), whole_spec((rows, 3 * D)), ANYWHERE],
            scratch_shapes=[
                pltpu.VMEM((TILES, TILE, LANES), jnp.bfloat16),
                pltpu.SemaphoreType.DMA((sum(len(listed) for listed in slots),)),
                pltpu.SemaphoreType.DMA(()),
            ],
        ),
        out_shape=[low_like(rows, D), low_like(rows, 3 * D), low_like(TILES, TILE, LANES)],
        compiler_params=PARAMS,
        name="project",
    )(position, *arrays, hidden, vectors)


def mlp_weights(tiles_ref, weight_ref, sems, order):
    copies = []
    for i, name in enumerate(order):
        depth, width = WEIGHTS[name]
        count = depth // TILE * (width // LANES)
        here = weight_ref.at[pl.ds(FIRST[name] - MLP_FIRST, count)]
        copies.append(pltpu.make_async_copy(tiles_ref.at[pl.ds(FIRST[name], count)], here, sems.at[i]))
        copies[-1].start()
    return copies


def span_of(step):
    return slice(step * SPAN, (step + 1) * SPAN)


class Leaving:
    def __init__(self, outs, buffers, sems):
        self.outs, self.buffers, self.sems, self.copies = outs, buffers, sems, []

    def start(self, number, columns=None):
        source, target = self.buffers[number], self.outs[number]
        if columns is not None:
            source, target = source.at[:, columns], target.at[:, columns]
        self.copies.append(pltpu.make_async_copy(source, target, self.sems.at[len(self.copies)]))
        self.copies[-1].start()

    def wait(self):
        for copy in self.copies:
            copy.wait()


def mlp_kernel(attended_ref, hidden_ref, vectors_ref, tiles_ref, *refs):
    outs, buffers, (total_ref, weight_ref, sems, out_sems, fc1_bias_ref) = refs[:7], refs[7:14], refs[14:]
    result_ref, branch_ref, middle_ref, normed_ref, activ_ref, slope_ref, mlp_ref = buffers
    leaving = Leaving(outs, buffers, out_sems)
    copies = mlp_weights(tiles_ref, weight_ref, sems, ("proj_weight", "fc1_weight", "fc2_weight"))
    fc1_bias_ref[...] = wide_row(vectors_ref, FC1_AT, FF // LANES)
    copies[0].wait()
    across = D // LANES
    weight = load_weight(weight_ref, MLP_FIRST, "proj_weight", 0, D // TILE, 0, across)
    branch = product(attended_ref[...], weight, NN) + vector(vectors_ref, "proj_bias")
    branch_ref[...] = branch.astype(jnp.bfloat16)
    leaving.start(1)
    middle_ref[...] = hidden_ref[...] + vector(vectors_ref, "gamma_attn") * branch
    leaving.start(2)
    normal, _ = norm_parts(middle_ref[...])
    normed_ref[...] = (normal * vector(vectors_ref, "norm2_gain") + vector(vectors_ref, "norm2_bias")).astype(
        jnp.bfloat16
    )
    leaving.start(3)
    total_ref[...] = jnp.broadcast_to(vector(vectors_ref, "fc2_bias"), total_ref.shape)
    copies[1].wait()

    def step(i, _):
        span = span_of(i)
        weight = load_weight(weight_ref, MLP_FIRST, "fc1_weight", 0, D // TILE, i * (SPAN // LANES), SPAN // LANES)
        activ, slope = gelu_and_slope(product(normed_ref[...], weight, NN) + fc1_bias_ref[:, span])
        activ = activ.astype(jnp.bfloat16)
        activ_ref[:, span] = activ
        slope_ref[:, span] = slope.astype(jnp.bfloat16)
        leaving.start(4, span)
        leaving.start(5, span)
        if i == 0:
            copies[2].wait()
        weight = load_weight(weight_ref, MLP_FIRST, "fc2_weight", i * (SPAN // TILE), SPAN // TILE, 0, across)
        total_ref[...] += product(activ, weight, NN)
        return 0

    for i in range(FF // SPAN):
        step(i, 0)
    result_ref[...] = middle_ref[...] + vector(vectors_ref, "gamma_mlp") * total_ref[...]
    leaving.start(0)
    mlp_ref[...] = total_ref[...].astype(jnp.bfloat16)
    leaving.start(6)
    leaving.wait()


def mlp_scratch(rows, outs):
    return [pltpu.VMEM(out.shape, out.dtype) for out in outs] + [
        pltpu.VMEM((rows, D), jnp.float32),
        pltpu.VMEM((TILES - MLP_FIRST, TILE, LANES), jnp.bfloat16),
        pltpu.SemaphoreType.DMA((3,)),
        pltpu.SemaphoreType.DMA((len(outs) + 2 * (FF // SPAN),)),
    ]


def mlp(attended, hidden, vectors, tiles):
    rows = hidden.shape[0]
    outs = [full_like(rows, D), low_like(rows, D), full_like(rows, D), low_like(rows, D)]
    outs += [low_like(rows, FF), low_like(rows, FF), low_like(rows, D)]
    ins = [attended, hidden, vectors]
    return pl.pallas_call(
        mlp_kernel,
        grid=(1,),
        in_specs=[whole_spec(array.shape) for array in ins] + [ANYWHERE],
        out_specs=[ANYWHERE] * len(outs),
        out_shape=outs,
        scratch_shapes=mlp_scratch(rows, outs) + [pltpu.VMEM((1, FF), jnp.float32)],
        compiler_params=PARAMS,
        name="mlp",
    )(*ins, tiles)


def mlp_back_kernel(grad_ref, branch_ref, middle_ref, slope_ref, mlp_ref, vectors_ref, tiles_ref, *refs):
    outs, buffers, (total_ref, weight_ref, sems, out_sems) = refs[:6], refs[6:12], refs[12:]
    grad_middle_ref, grad_attended_ref, grad_mlp_ref, grad_pre_ref, grad_branch_ref, sums_ref = buffers
    leaving = Leaving(outs, buffers, out_sems)
    copies = mlp_weights(tiles_ref, weight_ref, sems, ("fc2_weight", "fc1_weight", "proj_weight"))
    across = D // LANES
    grad = grad_ref[...]
    sums_ref[...] = jnp.zeros_like(sums_ref)
    put_vector(sums_ref, later_row("gamma_mlp"), grad * mlp_ref[...].astype(jnp.float32))
    grad_mlp = grad * vector(vectors_ref, "gamma_mlp")
    put_vector(sums_ref, later_row("fc2_bias"), grad_mlp)
    grad_mlp_ref[...] = grad_mlp.astype(jnp.bfloat16)
    leaving.start(2)
    total_ref[...] = jnp.zeros_like(total_ref)
    copies[0].wait()

    def step(i, _):
        span = span_of(i)
        weight = load_weight(weight_ref, MLP_FIRST, "fc2_weight", i * (SPAN // TILE), SPAN // TILE, 0, across)
        grad_pre = product(grad_mlp_ref[...], weight, NT) * slope_ref[:, span].astype(jnp.float32)
        sums = jnp.sum(grad_pre, axis=0, keepdims=True)
        sums = jnp.concatenate([sums[:, k * LANES : (k + 1) * LANES] for k in range(SPAN // LANES)], axis=0)
        first = FC1_AT - LATER * VECTOR_ROWS + i * (SPAN // LANES)
        sums_ref[first : first + SPAN // LANES] = sums
        grad_pre = grad_pre.astype(jnp.bfloat16)
        grad_pre_ref[:, span] = grad_pre
        leaving.start(3, span)
        if i == 0:
            copies[1].wait()
        weight = load_weight(weight_ref, MLP_FIRST, "fc1_weight", 0, D // TILE, i * (SPAN // LANES), SPAN // LANES)
        total_ref[...] += product(grad_pre, weight, NT)
        return 0

    for i in range(FF // SPAN):
        step(i, 0)
    normal, inverse = norm_parts(middle_ref[...])
    grad_normed = total_ref[...]
    put_vector(sums_ref, later_row("norm2_gain"), grad_normed * normal)
    put_vector(sums_ref, later_row("norm2_bias"), grad_normed)
    grad_middle = grad_ref[...] + norm_back(grad_normed, normal, inverse, vector(vectors_ref, "norm2_gain"))
    grad_middle_ref[...] = grad_middle
    leaving.start(0)
    put_vector(sums_ref, later_row("gamma_attn"), grad_middle * branch_ref[...].astype(jnp.float32))
    grad_branch = grad_middle * vector(vectors_ref, "gamma_attn")
    put_vector(sums_ref, later_row("proj_bias"), grad_branch)
    leaving.start(5)
    grad_branch_ref[...] = grad_branch.astype(jnp.bfloat16)
    leaving.start(4)
    copies[2].wait()
    weight = load_weight(weight_ref, MLP_FIRST, "proj_weight", 0, D // TILE, 0, across)
    grad_attended_ref[...] = product(grad_branch_ref[...], weight, NT).astype(jnp.bfloat16)
    leaving.start(1)
    leaving.wait()


def mlp_back(grad, saved, vectors, tiles):
    rows = grad.shape[0]
    outs = [full_like(rows, D), low_like(rows, D), low_like(rows, D), low_like(rows, FF), low_like(rows, D)]
    outs += [full_like(TABLE_AT - LATER * VECTOR_ROWS, LANES)]
    ins = [grad, saved["branch"], saved["middle"], saved["slope"], saved["mlp_out"], vectors]
    return pl.pallas_call(
        mlp_back_kernel,
        grid=(1,),
        in_specs=[whole_spec(array.shape) for array in ins] + [ANYWHERE],
        out_specs=[ANYWHERE] * len(outs),
        out_shape=outs,
        scratch_shapes=mlp_scratch(rows, outs),
        compiler_params=PARAMS,
        name="mlp_back",
    )(*ins, tiles)


def scatter_place(places, at_ref, device, part):
    position = np.unravel_index(device, places.grid.shape)
    apart = {name: at_ref[i] ^ int(position[i]) for name, i in places.axis.items()}
    first, second = ORDERS[part]
    slot = (apart[first] * places.sizes[second] + apart[second]) * places.sizes["z"] + apart["z"]
    return apart["c"], slot


def weight_back_kernel(places, stepwise, at_ref, *refs):
    sources, refs = refs[:8], refs[8:]
    outs = refs[: 2 * places.sizes["c"] if stepwise else 1]
    operands, (whole_ref, in_sems, sems) = refs[len(outs) : len(outs) + 8], refs[len(outs) + 8 :]
    coming = [
        pltpu.make_async_copy(source, operand, in_sems.at[i]) for i, (source, operand) in enumerate(zip(sources, operands))
    ]
    for copy in coming:
        copy.start()
    normed_ref, project_ref, attended_ref, branch_ref, normed2_ref, pre_ref, activ_ref, mlp_ref = operands
    across = D // LANES

    def put(name, row, column, left, grad):
        block = product(left, grad, TN).astype(jnp.bfloat16)
        wide = WEIGHTS[name][1] // LANES
        for i in range(D // TILE):
            for j in range(across):
                at = FIRST[name] + (row + i) * wide + column + j
                whole_ref[at] = block[i * TILE : (i + 1) * TILE, j * LANES : (j + 1) * LANES]

    half = TILES // places.count // 2
    sent = []

    def send(ready):
        while stepwise and (len(sent) + 1) * half <= ready:
            number = len(sent)
            core, slot = scatter_place(places, at_ref, number // 2, number % 2)
            source = whole_ref.at[pl.ds(number * half, half)]
            for k in range(places.sizes["c"]):
                target = outs[number % 2 * places.sizes["c"] + k].at[pl.ds(slot * half, half)]
                copy = pltpu.make_async_copy(source, target, sems.at[number])
                pl.when(core == k)(copy.start)
            sent.append(copy)

    coming[0].wait()
    coming[1].wait()
    for part in range(3):
        put("qkv_weight", 0, part * across, normed_ref[...], project_ref[part])
    send(FIRST["proj_weight"])
    coming[2].wait()
    coming[3].wait()
    put("proj_weight", 0, 0, attended_ref[...], branch_ref[...])
    send(FIRST["fc1_weight"])
    coming[4].wait()
    coming[5].wait()
    for part in range(FF // D):
        put("fc1_weight", 0, part * across, normed2_ref[...], pre_ref[:, part * D : (part + 1) * D])
    send(FIRST["fc2_weight"])
    coming[6].wait()
    coming[7].wait()
    for part in range(FF // D):
        put("fc2_weight", part * (D // TILE), 0, activ_ref[:, part * D : (part + 1) * D], mlp_ref[...])
        send(FIRST["fc2_weight"] + (part + 1) * (D // TILE) * across)
    if not stepwise:
        sent.append(pltpu.make_async_copy(whole_ref, outs[0], sems.at[0]))
        sent[0].start()
    for copy in sent:
        copy.wait()


def weight_back(places, position, stepwise, ins):
    cores = places.sizes["c"]
    counts = [TILES // (2 * cores)] * (2 * cores) if stepwise else [TILES]
    return pl.pallas_call(
        functools.partial(weight_back_kernel, places, stepwise),
        grid_spec=pltpu.PrefetchScalarGridSpec(
            num_scalar_prefetch=1,
            grid=(1,),
            in_specs=[ANYWHERE] * len(ins),
            out_specs=[ANYWHERE] * len(counts),
            scratch_shapes=[pltpu.VMEM(array.shape, array.dtype) for array in ins]
            + [
                pltpu.VMEM((TILES, TILE, LANES), jnp.bfloat16),
                pltpu.SemaphoreType.DMA((len(ins),)),
                pltpu.SemaphoreType.DMA((2 * places.count,)),
            ],
        ),
        out_shape=[low_like(count, TILE, LANES) for count in counts],
        compiler_params=PARAMS,
        name="weight_back",
    )(position, *ins)


def input_back_kernel(project_ref, grad_middle_ref, hidden_ref, vectors_ref, tiles_ref, out_ref, sums_ref, total_ref):
    across = D // LANES
    for part in range(3):
        weight = load_weight(tiles_ref, 0, "qkv_weight", 0, D // TILE, part * across, across)
        rows = product(project_ref[part], weight, NT)
        total_ref[...] = rows if part == 0 else total_ref[...] + rows
    normal, inverse = norm_parts(hidden_ref[...])
    grad_normed = total_ref[...]
    put_vector(sums_ref, 0, grad_normed * normal)
    put_vector(sums_ref, VECTOR_ROWS, grad_normed)
    put_vector(sums_ref, 2 * VECTOR_ROWS, project_ref[0].astype(jnp.float32))
    put_vector(sums_ref, 3 * VECTOR_ROWS, project_ref[2].astype(jnp.float32))
    out_ref[...] = grad_middle_ref[...] + norm_back(
        grad_normed, normal, inverse, vector(vectors_ref, "norm1_gain")
    )


def input_back(grad_project, grad_middle, hidden, vectors, tiles):
    rows = hidden.shape[0]
    ins = [grad_project, grad_middle, hidden, vectors]
    return pl.pallas_call(
        input_back_kernel,
        grid=(1,),
        in_specs=[whole_spec(array.shape) for array in ins] + [whole_spec((MLP_FIRST, TILE, LANES))],
        out_specs=[whole_spec((rows, D)), whole_spec((LATER * VECTOR_ROWS, LANES))],
        out_shape=[full_like(rows, D), full_like(LATER * VECTOR_ROWS, LANES)],
        scratch_shapes=[pltpu.VMEM((rows, D), jnp.float32)],
        compiler_params=PARAMS,
        name="input_back",
    )(*ins, tiles)


def pad_rows(images):
    padded = jnp.pad(images, ((0, 0), (0, ROWS - SEQ), (0, 0)))
    return padded.reshape(-1, D).astype(jnp.float32)


def cut_rows(rows):
    return rows.reshape(-1, ROWS, D)[:, :SEQ].astype(jnp.bfloat16)


class Places:
    def __init__(self, dp, fsdp):
        low = 2 if dp % 2 == 0 else 1
        core = 2 if fsdp % 2 == 0 else 1
        self.sizes = {"y": low, "x": dp // low, "z": fsdp // core, "c": core}
        self.count = dp * fsdp
        grid = np.arange(self.count).reshape(tuple(self.sizes.values()))
        self.grid = grid
        self.axis = {name: i for i, name in enumerate(self.sizes)}

    def exchange(self, block, axis, hop):
        size = self.sizes[axis]
        target = np.take(self.grid, np.arange(size) ^ hop, axis=self.axis[axis])
        perm = [(int(a), int(b)) for a, b in zip(self.grid.reshape(-1), target.reshape(-1))]
        return lax.ppermute(block, AXES, perm)

    def hops(self, axis):
        return range(1, self.sizes[axis])

    def powers(self, axis):
        return [1 << bit for bit in range(self.sizes[axis].bit_length() - 1)]

    def total(self, block, axes):
        for axis in axes:
            for hop in self.powers(axis):
                block = block + self.exchange(block, axis, hop)
        return block

    def position(self, me):
        return jnp.stack([(me // int(np.prod(self.grid.shape[i + 1 :]))) % n for i, n in enumerate(self.grid.shape)])


def block_at(at_ref, places, offset):
    number = 0
    for i, size in enumerate(places.grid.shape):
        number = number * size + (at_ref[i] ^ offset[i])
    return number


def copies_in(places, at_ref, parts, slots, whole_ref, sems):
    copies = []
    for part, listed in zip(parts, slots):
        count = part.shape[0] // len(listed)
        for i, slot in enumerate(listed):
            start = 0 if slot is None else block_at(at_ref, places, slot[0]) * (TILES // places.count) + slot[1]
            target = whole_ref.at[pl.ds(start, count)]
            copies.append(pltpu.make_async_copy(part.at[pl.ds(i * count, count)], target, sems.at[len(copies)]))
    return copies


def offset_of(**hops):
    return tuple(hops.get(axis, 0) for axis in ("y", "x", "z", "c"))


def join(blocks):
    return jnp.concatenate(blocks, axis=0) if len(blocks) > 1 else blocks[0]


ORDERS = (("x", "y"), ("y", "x"))


def group_of(shares, offsets):
    half = shares[0].shape[0] // 2
    return [(join([share[part * half : (part + 1) * half] for share in shares]), offsets) for part in range(2)]


def merge(*groups):
    return [(join([group[part][0] for group in groups]), sum((group[part][1] for group in groups), [])) for part in range(2)]


def fetch_column(places, share):
    return [places.exchange(share, "z", hop) for hop in places.hops("z")]


def column_offsets(places):
    return [offset_of(z=hop) for hop in range(places.sizes["z"])]


def fetch_plane(places, group, step):
    arrived = []
    for (block, offsets), order in zip(group, ORDERS):
        at = places.axis[order[step]]
        hops = range(1, places.sizes[order[step]])
        moved = [offset[:at] + (hop,) + offset[at + 1 :] for hop in hops for offset in offsets]
        arrived.append((join([places.exchange(block, order[step], hop) for hop in hops]), moved))
    return arrived


def fetch_plane_with(places, group, step, rows):
    (block, offsets), order = group[0], ORDERS[0]
    count, axis = block.shape[0], order[step]
    hops = range(1, places.sizes[axis])
    arrived = [places.exchange(jnp.concatenate([block, rows], axis=0), axis, hop) for hop in hops]
    moved = [tuple(hop if i == places.axis[axis] else part for i, part in enumerate(o)) for hop in hops for o in offsets]
    rows = sum([piece[count:] for piece in arrived], rows)
    other = fetch_plane(places, group, step)[1]
    return [(join([piece[:count] for piece in arrived]), moved), other], rows


def list_core(places, groups):
    parts = []
    for group in groups:
        half = TILES // places.count // 2
        parts += [(block, [(offset, part * half) for offset in offsets]) for part, (block, offsets) in enumerate(group)]
    return parts


def gather_core(places, groups):
    parts = list_core(places, groups)
    return [(join([block for block, _ in parts]), sum((slots for _, slots in parts), []))]


def fetch_core(places, parts):
    arrived = []
    for hop in range(1, places.sizes["c"]):
        for block, slots in parts:
            moved = [(offset[:3] + (hop,), first) for offset, first in slots]
            arrived.append((places.exchange(block, "c", hop), moved))
    return parts + arrived


def add_low(*blocks):
    total = blocks[0].astype(jnp.float32)
    for block in blocks[1:]:
        total = total + block.astype(jnp.float32)
    return total


def send_core(places, parts):
    cores = places.sizes["c"]
    halves = [parts[:cores], parts[cores:]]
    return [[mine] + [places.exchange(other, "c", hop) for hop, other in enumerate(others, 1)] for mine, *others in halves]


def plane_totals(places, blocks, axis):
    share = blocks[0].shape[0] // places.sizes[axis]
    cuts = [slice(i * share, (i + 1) * share) for i in range(places.sizes[axis])]
    return [add_low(*[block[cut] for block in blocks]).astype(jnp.bfloat16) for cut in cuts]


def send_totals(places, totals, axis):
    return totals[:1] + [places.exchange(total, axis, hop) for hop, total in enumerate(totals[1:], 1)]


def send_plane(places, sums, step):
    axes = [order[step] for order in ORDERS]
    return [send_totals(places, plane_totals(places, blocks, axis), axis) for blocks, axis in zip(sums, axes)]


def send_plane_tied(places, sums, step, later):
    (first, second), axes = sums, [order[step] for order in ORDERS]
    first, later = tie(first, later)
    first = plane_totals(places, first, axes[0])
    second, first, later = tie(second, first, later)
    result = [send_totals(places, first, axes[0])]
    second, later = tie(plane_totals(places, second, axes[1]), later)
    return result + [send_totals(places, second, axes[1])], later


def column_totals(places, sums):
    count = places.sizes["z"]
    share = sums[0][0].shape[0] // count
    cuts = [slice(hop * share, (hop + 1) * share) for hop in range(count)]
    return [join([add_low(*[block[cut] for block in blocks]).astype(jnp.bfloat16) for blocks in sums]) for cut in cuts]


def send_column(places, totals):
    return [totals[0]] + [places.exchange(total, "z", hop) for hop, total in enumerate(totals[1:], 1)]


class Layer:
    def __init__(self, places, position, counts, vectors):
        self.places, self.position, self.counts, self.vectors = places, position, counts, vectors

    def project(self, hidden, parts):
        normed, qkv, tiles = project(self.places, self.position, parts, hidden, self.vectors)
        self.saved = dict(hidden=hidden, normed=normed, qkv=qkv, tiles=tiles)

    def forward(self):
        saved = self.saved
        saved["attended"], saved["weights"] = attention(self.counts, saved["qkv"], self.bias)
        names = ("branch", "middle", "normed2", "activ", "slope", "mlp_out")
        result, *kept = mlp(saved["attended"], saved["hidden"], self.vectors, saved["tiles"])
        saved.update(zip(names, kept))
        return result

    def back_mlp(self, grad):
        return mlp_back(grad, self.saved, self.vectors, self.saved["tiles"])

    def back_attention(self, passed):
        return attention_back(self.saved["qkv"], passed[1], self.saved["weights"])

    def back_weights(self, passed, grad_project, stepwise):
        _, _, grad_mlp, grad_pre, grad_branch, _ = passed
        saved = self.saved
        ins = [saved["normed"], grad_project, saved["attended"], grad_branch, saved["normed2"], grad_pre]
        return weight_back(self.places, self.position, stepwise, ins + [saved["activ"], grad_mlp])

    def back_input(self, passed, grad_project):
        return input_back(grad_project, passed[0], self.saved["hidden"], self.vectors, self.saved["tiles"])


def scatter_whole(parts):
    whole = parts[0].reshape(-1, LANES)
    return lax.psum_scatter(whole, AXES, scatter_dimension=0, tiled=True).astype(jnp.float32)


def local(dp, fsdp, tokens, counts, params_first, params_second, cotangent):
    devices = dp * fsdp
    places = Places(dp, fsdp)
    stepwise = TILES % (4 * devices) == 0 and all(size & (size - 1) == 0 for size in places.sizes.values())
    share_rows = TILES * TILE // devices
    me = lax.axis_index(AXES)
    position = places.position(me)
    owned = Owned([params_first, params_second], me, devices)
    own = owned.share(0)
    small_rows = owned.small_rows(own)
    hidden, grad_output = pad_rows(tokens), pad_rows(cotangent)

    if stepwise:
        own = own.reshape(-1, TILE, LANES)
        column = fetch_column(places, own)
        near, small_rows = tie(group_of([own], [offset_of()]), small_rows)
        small_rows = small_rows.reshape(-1, TILE, LANES)
        near_first, small_rows = fetch_plane_with(places, near, 0, small_rows)
        near_first, small_rows = tie(near_first, small_rows)
        near_second, small_rows = fetch_plane_with(places, merge(near, near_first), 1, small_rows)
        small_rows = places.total(small_rows, "c")
        next_own, near_first = tie(owned.share(1, own), near_first)
        far, near_second = tie(group_of(column, column_offsets(places)[1:]), near_second)
        far_first = fetch_plane(places, far, 0)
        next_own, small_rows, far, hidden, grad_output = tie(next_own, small_rows, far, hidden, grad_output)
        next_own = jnp.concatenate([next_own, small_rows.reshape(-1, LANES)], axis=0)
        next_shares = [next_own] + fetch_column(places, next_own)
        small_rows = sum([rows[share_rows:] for rows in next_shares[1:]], next_own[share_rows:])
        small_rows = small_rows.reshape(2, -1, LANES)
        vectors = small_rows.astype(jnp.float32)
        next_shares = [rows[:share_rows].reshape(-1, TILE, LANES) for rows in next_shares]
        group = group_of(next_shares, column_offsets(places))
        far_second = fetch_plane(places, merge(far, far_first), 1)
        early = gather_core(places, [near, near_first, near_second, far, far_first])
    else:
        small_rows = lax.psum(small_rows, AXES)
    if stepwise:
        far_second, early, group, small_rows, vectors = tie(far_second, early, group, small_rows, vectors)
        first = fetch_plane(places, group, 0)
        parts = fetch_core(places, early) + fetch_core(places, list_core(places, [far_second]))
        entries = table_entries(small_rows)
        first_layer = Layer(places, position, counts, vectors[0])
        first_layer.bias, second_bias = bias_of(entries[0]), bias_of(entries[1])
        first, group, parts, first_layer.bias, second_bias = tie(first, group, parts, first_layer.bias, second_bias)
        second_group = merge(group, first)
        second = fetch_plane(places, second_group, 1)
        parts, _ = tie(parts, second_group)
        next_parts = fetch_core(places, list_core(places, [first]))
        first_layer.project(hidden, parts)
        result = first_layer.forward()
        next_parts, result = tie(next_parts, result)
        next_parts += fetch_core(places, gather_core(places, [group]))
        second, next_parts, result, second_bias = tie(second, next_parts, result, second_bias)
        next_parts += fetch_core(places, list_core(places, [second]))
    else:
        vectors = small_rows.astype(jnp.float32)
        entries = table_entries(small_rows)
        second_bias = bias_of(entries[1])
        parts, next_parts = [
            [(lax.all_gather(share, AXES, axis=0, tiled=True).reshape(TILES, TILE, LANES), [None])]
            for share in (own, owned.share(1))
        ]
        first_layer = Layer(places, position, counts, vectors[0])
        first_layer.project(hidden, parts)
        first_layer.bias = bias_of(entries[0])
        result = first_layer.forward()
    second_layer = Layer(places, position, counts, vectors[1])
    second_layer.bias = second_bias
    second_layer.project(result, next_parts)
    result = second_layer.forward()
    output = cut_rows(result)

    next_passed = second_layer.back_mlp(grad_output)
    next_project, next_bias = second_layer.back_attention(next_passed)
    parts = second_layer.back_weights(next_passed, next_project, stepwise)
    if stepwise:
        sums = send_core(places, parts)
    else:
        next_share = scatter_whole(parts)
    grad, next_sums = second_layer.back_input(next_passed, next_project)
    if stepwise:
        sums, grad = send_plane_tied(places, sums, 0, grad)
    passed = first_layer.back_mlp(grad)
    project_grad, bias = first_layer.back_attention(passed)
    parts = first_layer.back_weights(passed, project_grad, stepwise)
    if stepwise:
        sums, parts, passed, project_grad = tie(sums, parts, passed, project_grad)
        sums = send_plane(places, sums, 1)
        own_sums = send_core(places, parts)
    else:
        share = scatter_whole(parts)
    if stepwise:
        own_sums, later = send_plane_tied(places, own_sums, 0, (bias, passed, project_grad))
        sums, (bias, passed, project_grad) = tie(sums, later)
        sums = send_column(places, column_totals(places, sums))
    grad, own_row_sums = first_layer.back_input(passed, project_grad)
    small_grads = small_gradients(
        [own_row_sums, next_sums], [passed[5], next_passed[5]], tables_from_biases(bias, next_bias)
    )
    flat_share = FlatShare(me, devices, params_first.shape[0] * devices)
    if stepwise:
        own_sums, sums, small_grads = tie(own_sums, sums, small_grads)
        own_sums = send_plane(places, own_sums, 1)
        small_grads = places.total(small_grads, "zc")
        own_sums, small_grads = tie(own_sums, small_grads)
        own_sums = send_column(places, column_totals(places, own_sums))
        small_grads = places.total(small_grads, "xy")
        small_grads, sums = tie(small_grads, sums)
        grad_second = flat_share(add_low(*sums).reshape(-1, LANES), small_grads[1])
        own_sums, grad_second, output, grad_tokens = tie(own_sums, grad_second, output, cut_rows(grad))
        share = add_low(*own_sums).reshape(-1, LANES)
    else:
        small_grads = lax.psum(small_grads, AXES)
        grad_second = flat_share(next_share, small_grads[1])
        grad_tokens = cut_rows(grad)
    grad_first = flat_share(share, small_grads[0])
    return output, grad_tokens, grad_first, grad_second


def solution(mesh):
    return jax.shard_map(
        functools.partial(local, mesh.shape["dp"], mesh.shape["fsdp"]),
        mesh=mesh,
        in_specs=(P(AXES, None, None), P(AXES), P(AXES), P(AXES), P(AXES, None, None)),
        out_specs=(P(AXES, None, None), P(AXES, None, None), P(AXES), P(AXES)),
        check_vma=False,
    )
```

profile of v0, /device:TPU:11, one launch (start us, length us, event | category | flops | bytes accessed | tf_op | source)
XLA Modules:
  0.0 477.8 jit_solution(2471935068507353242)
XLA Ops:
  41.3 18.1 %collective-permute-done.7 = bf16[108,16,128]{2,1,0:T(8,128)(2,1)S(1)} collective-permute-done((bf16[108,16,128]{2,1,0:T(8,128)(2,1)S(1)}, bf16[108,16,128]{2,1,0:T(8,128)(2,1)S(1)}, u32[]{:S(2)}, u32[]{:S(2)}) %collective-permute-start.7) | collective-permute-done | bytes 442400 | tf_op jit(solution)/shard_map/ppermute | solution.py:902
  59.4 8.4 %collective-permute-done.8 = bf16[108,16,128]{2,1,0:T(8,128)(2,1)S(1)} collective-permute-done((bf16[108,16,128]{2,1,0:T(8,128)(2,1)S(1)}, bf16[108,16,128]{2,1,0:T(8,128)(2,1)S(1)}, u32[]{:S(2)}, u32[]{:S(2)}) %collective-permute-start.8) | collective-permute-done | bytes 442400 | tf_op jit(solution)/shard_map/ppermute | solution.py:902
  77.5 8.7 %collective-permute-done.12 = bf16[162,16,128]{2,1,0:T(8,128)(2,1)S(1)} collective-permute-done((bf16[162,16,128]{2,1,0:T(8,128)(2,1)S(1)}, bf16[162,16,128]{2,1,0:T(8,128)(2,1)S(1)}, u32[]{:S(2)}, u32[]{:S(2)}) %collective-permute-start.12) | collective-permute-done | bytes 663584 | tf_op jit(solution)/shard_map/ppermute | solution.py:902
  88.1 6.2 %collective-permute-done.14 = bf16[2048,128]{1,0:T(8,128)(2,1)S(1)} collective-permute-done((bf16[2048,128]{1,0:T(8,128)(2,1)S(1)}, bf16[2048,128]{1,0:T(8,128)(2,1)S(1)}, u32[]{:S(2)}, u32[]{:S(2)}) %collective-permute-start.14) | collective-permute-done | bytes 524320 | tf_op jit(solution)/shard_map/ppermute | solution.py:902
  97.8 22.7 %collective-permute-done.16 = bf16[2048,128]{1,0:T(8,128)(2,1)S(1)} collective-permute-done((bf16[2048,128]{1,0:T(8,128)(2,1)S(1)}, bf16[2048,128]{1,0:T(8,128)(2,1)S(1)}, u32[]{:S(2)}, u32[]{:S(2)}) %collective-permute-start.16) | collective-permute-done | bytes 524320 | tf_op jit(solution)/shard_map/ppermute | solution.py:902
  138.6 8.4 %collective-permute-done.17.refs_0_ = bf16[216,16,128]{2,1,0:T(8,128)(2,1)} collective-permute-done((bf16[216,16,128]{2,1,0:T(8,128)(2,1)S(1)}, bf16[216,16,128]{2,1,0:T(8,128)(2,1)}, u32[]{:S(2)}, u32[]{:S(2)}) %collective-permute-start.17) | collective-permute-done | bytes 884768 | tf_op jit(solution)/shard_map/ppermute | solution.py:902
  159.0 14.2 %project.2 = (bf16[416,768]{1,0:T(8,128)(2,1)}, bf16[416,2304]{1,0:T(8,128)(2,1)}, bf16[3456,16,128]{2,1,0:T(8,128)(2,1)}) custom-call(s32[4]{0:T(128)} %pad_add_fusion.at_ref, bf16[1080,16,128]{2,1,0:T(8,128)(2,1)} %constant_dynamic-update-slice_fusion.refs_0_, bf16[1080,16,128]{2,1,0:T(8,128)(2,1)} %collective-permute-done.19.refs_1_, ...), custom_call_target="tpu_custom_call" | custom-call | tf_op jit(solution)/shard_map/project/pallas_call | solution.py:562
  173.2 7.4 %attention.2 = (bf16[416,768]{1,0:T(8,128)(2,1)}, bf16[2,12,208,208]{3,2,1,0:T(8,128)(2,1)}) custom-call(s32[2]{0:T(128)} %counts_ref.3, bf16[416,2304]{1,0:T(8,128)(2,1)} %get-tuple-element.236.query_ref.key_ref.value_ref, bf16[416,2304]{1,0:T(8,128)(2,1)} %get-tuple-element.236.query_ref.key_ref.value_ref, ...), custom_call_target="tpu_custom_call" | custom-call | tf_op jit(solution)/shard_map/attention/pallas_call | solution.py:413
  180.7 13.3 %mlp.2 = (f32[416,768]{1,0:T(8,128)}, bf16[416,768]{1,0:T(8,128)(2,1)}, f32[416,768]{1,0:T(8,128)}, bf16[416,768]{1,0:T(8,128)(2,1)}, bf16[416,3072]{1,0:T(8,128...) custom-call(bf16[416,768]{1,0:T(8,128)(2,1)} %get-tuple-element.238.attended_ref.refs_2_, ...), custom_call_target="tpu_custom_call" | custom-call | tf_op jit(solution)/shard_map/mlp/pallas_call | solution.py:672
  204.7 14.2 %project.3 = (bf16[416,768]{1,0:T(8,128)(2,1)}, bf16[416,2304]{1,0:T(8,128)(2,1)}, bf16[3456,16,128]{2,1,0:T(8,128)(2,1)}) custom-call(s32[4]{0:T(128)} %pad_add_fusion.at_ref, bf16[216,16,128]{2,1,0:T(8,128)(2,1)} %collective-permute-done.17.refs_0_, bf16[216,16,128]{2,1,0:T(8,128)(2,1)} %collective-permute-done.18.refs_1_, ...), custom_call_target="tpu_custom_call" | custom-call | tf_op jit(solution)/shard_map/project/pallas_call | solution.py:562
  218.9 7.8 %attention.3 = (bf16[416,768]{1,0:T(8,128)(2,1)}, bf16[2,12,208,208]{3,2,1,0:T(8,128)(2,1)}) custom-call(s32[2]{0:T(128)} %counts_ref.3, bf16[416,2304]{1,0:T(8,128)(2,1)} %get-tuple-element.257.query_ref.key_ref.value_ref, bf16[416,2304]{1,0:T(8,128)(2,1)} %get-tuple-element.257.query_ref.key_ref.value_ref, ...), custom_call_target="tpu_custom_call" | custom-call | tf_op jit(solution)/shard_map/attention/pallas_call | solution.py:413
  226.8 13.2 %mlp.3 = (f32[416,768]{1,0:T(8,128)}, bf16[416,768]{1,0:T(8,128)(2,1)}, f32[416,768]{1,0:T(8,128)}, bf16[416,768]{1,0:T(8,128)(2,1)}, bf16[416,3072]{1,0:T(8,128...) custom-call(bf16[416,768]{1,0:T(8,128)(2,1)} %get-tuple-element.260.attended_ref.refs_2_, ...), custom_call_target="tpu_custom_call" | custom-call | tf_op jit(solution)/shard_map/mlp/pallas_call | solution.py:672
  240.0 13.3 %mlp_back.2 = (f32[416,768]{1,0:T(8,128)}, bf16[416,768]{1,0:T(8,128)(2,1)}, bf16[416,768]{1,0:T(8,128)(2,1)}, bf16[416,3072]{1,0:T(8,128)(2,1)}, bf16[416,768]{1,0:T(8,128)(2,1)}, /*index=5*/f32[64,128]{1,0:T(8,128)}) custom-call(f32[416,768]{1,0:T(8,128)} %bitcast.86, bf16[416,768]{1,0:T(8,128)(2,1)} %get-tuple-element.262.branch_ref, ...), custom_call_target="tpu_custom_call" | custom-call | tf_op jit(solution)/shard_map/mlp_back/pallas_call | solution.py:744
  253.3 10.8 %attention_back.2 = (bf16[3,416,768]{2,1,0:T(8,128)(2,1)}, f32[12,208,208]{2,1,0:T(8,128)}) custom-call(bf16[416,2304]{1,0:T(8,128)(2,1)} %get-tuple-element.257.query_ref.key_ref.value_ref, bf16[416,2304]{1,0:T(8,128)(2,1)} %get-tuple-element.257.query_ref.key_ref.value_ref, bf16[416,2304]{1,0:T(8,128)(2,1)} %get-tuple-element.257.query_ref.key_ref.value_ref, ...), custom_call_target="tpu_custom_call" | custom-call | tf_op jit(solution)/shard_map/attention_back/pallas_call | solution.py:433
  264.1 12.9 %weight_back.2 = (bf16[864,16,128]{2,1,0:T(8,128)(2,1)}, bf16[864,16,128]{2,1,0:T(8,128)(2,1)}, bf16[864,16,128]{2,1,0:T(8,128)(2,1)}, bf16[864,16,128]{2,1,0:T(8,128)(2,1)}) custom-call(s32[4]{0:T(128)} %pad_add_fusion.at_ref, bf16[416,768]{1,0:T(8,128)(2,1)} %get-tuple-element.256.refs_0_, bf16[3,416,768]{2,1,0:T(8,128)(2,1)} %get-tuple-element.268.refs_1_.project_ref, ...), custom_call_target="tpu_custom_call" | custom-call | tf_op jit(solution)/shard_map/weight_back/pallas_call | solution.py:827
  277.5 6.7 %input_back.2 = (f32[416,768]{1,0:T(8,128)}, f32[24,128]{1,0:T(8,128)}) custom-call(bf16[3,416,768]{2,1,0:T(8,128)(2,1)} %get-tuple-element.268.refs_1_.project_ref, f32[416,768]{1,0:T(8,128)} %get-tuple-element.278.grad_middle_ref, f32[416,768]{1,0:T(8,128)} %get-tuple-element.255.refs_10_.hidden_ref, f32[160,128]{1,0:T(8,128)} %get-tuple-element.432.refs_11_.vectors_ref, ...), custom_call_target="tpu_custom_call" | custom-call | tf_op jit(solution)/shard_map/input_back/pallas_call | solution.py:867
  292.8 13.1 %mlp_back.3 = (f32[416,768]{1,0:T(8,128)}, bf16[416,768]{1,0:T(8,128)(2,1)}, bf16[416,768]{1,0:T(8,128)(2,1)}, bf16[416,3072]{1,0:T(8,128)(2,1)}, bf16[416,768]{1,0:T(8,128)(2,1)}, /*index=5*/f32[64,128]{1,0:T(8,128)}) custom-call(f32[416,768]{1,0:T(8,128)} %get-tuple-element.291.grad_ref, bf16[416,768]{1,0:T(8,128)(2,1)} %get-tuple-element.292.branch_ref, ...), custom_call_target="tpu_custom_call" | custom-call | tf_op jit(solution)/shard_map/mlp_back/pallas_call | solution.py:744
  306.0 10.8 %attention_back.3 = (bf16[3,416,768]{2,1,0:T(8,128)(2,1)}, f32[12,208,208]{2,1,0:T(8,128)}) custom-call(bf16[416,2304]{1,0:T(8,128)(2,1)} %get-tuple-element.236.query_ref.key_ref.value_ref, bf16[416,2304]{1,0:T(8,128)(2,1)} %get-tuple-element.236.query_ref.key_ref.value_ref, bf16[416,2304]{1,0:T(8,128)(2,1)} %get-tuple-element.236.query_ref.key_ref.value_ref, ...), custom_call_target="tpu_custom_call" | custom-call | tf_op jit(solution)/shard_map/attention_back/pallas_call | solution.py:433
  316.8 12.9 %weight_back.3 = (bf16[864,16,128]{2,1,0:T(8,128)(2,1)}, bf16[864,16,128]{2,1,0:T(8,128)(2,1)}, bf16[864,16,128]{2,1,0:T(8,128)(2,1)}, bf16[864,16,128]{2,1,0:T(8,128)(2,1)}) custom-call(s32[4]{0:T(128)} %pad_add_fusion.at_ref, bf16[416,768]{1,0:T(8,128)(2,1)} %get-tuple-element.290.refs_0_, bf16[3,416,768]{2,1,0:T(8,128)(2,1)} %get-tuple-element.346.refs_1_.project_ref, ...), custom_call_target="tpu_custom_call" | custom-call | tf_op jit(solution)/shard_map/weight_back/pallas_call | solution.py:827
  348.8 6.5 %collective-permute-done.38 = bf16[216,16,128]{2,1,0:T(8,128)(2,1)S(1)} collective-permute-done((bf16[216,16,128]{2,1,0:T(8,128)(2,1)S(1)}, bf16[216,16,128]{2,1,0:T(8,128)(2,1)S(1)}, u32[]{:S(2)}, u32[]{:S(2)}) %collective-permute-start.38) | collective-permute-done | bytes 884768 | tf_op jit(solution)/shard_map/ppermute | solution.py:902
  362.4 14.9 %table_back.1 = f32[32,768]{1,0:T(8,128)} custom-call(f32[12,208,208]{2,1,0:T(8,128)} %get-tuple-element.352.first_ref, f32[12,208,208]{2,1,0:T(8,128)} %get-tuple-element.353.second_ref), custom_call_target="tpu_custom_call" | custom-call | tf_op jit(solution)/shard_map/table_back/pallas_call | solution.py:319
  382.6 6.6 %input_back.3 = (f32[416,768]{1,0:T(8,128)}, f32[24,128]{1,0:T(8,128)}) custom-call(bf16[3,416,768]{2,1,0:T(8,128)(2,1)} %get-tuple-element.346.refs_1_.project_ref, f32[416,768]{1,0:T(8,128)} %get-tuple-element.347.grad_middle_ref, f32[416,768]{1,0:T(8,128)} %bitcast.85, f32[160,128]{1,0:T(8,128)} %get-tuple-element.433.refs_7_.vectors_ref, ...), custom_call_target="tpu_custom_call" | custom-call | tf_op jit(solution)/shard_map/input_back/pallas_call | solution.py:867
  428.2 8.1 %collective-permute-start.52 = (bf16[384,128]{1,0:T(8,128)(2,1)S(1)}, bf16[384,128]{1,0:T(8,128)(2,1)S(1)}, u32[]{:S(2)}, u32[]{:S(2)}) collective-permute-start(bf16[384,128]{1,0:T(8,128)(2,1)S(1)} %bitcast.124), channel_id=1, source_target_pairs={{0,1},{1,2},{2,3},{3,4},{4,5},{5,6},{6,7},{7,8},{8,9},{9,10},{10,1... | collective-permute-start | bytes 294920 | tf_op jit(solution)/shard_map/ppermute | solution.py:116
  441.0 20.1 %collective-permute-done.53 = bf16[288,128]{1,0:T(8,128)(2,1)S(1)} collective-permute-done((bf16[288,128]{1,0:T(8,128)(2,1)S(1)}, bf16[288,128]{1,0:T(8,128)(2,1)S(1)}, u32[]{:S(2)}, u32[]{:S(2)}) %collective-permute-start.53) | collective-permute-done | bytes 73760 | tf_op jit(solution)/shard_map/ppermute | solution.py:120
  (266 shorter events, 196.8 us)
Async XLA Ops:
  24.7 34.7 %collective-permute-start.7 = (bf16[108,16,128]{2,1,0:T(8,128)(2,1)S(1)}, bf16[108,16,128]{2,1,0:T(8,128)(2,1)S(1)}, u32[]{:S(2)}, u32[]{:S(2)}) collective-permute-start(bf16[108,16,128]{2,1,0:T(8,128)(2,1)S(1)} %bitcast.118), channel_id=1, source_target_pairs={{0,4},{1,5},{2,6},{3,7},{4,0},{5,1},{6,2},{7,3},{8,12},{9,13},{10,... | collective-permute-start | bytes 1327112 | tf_op jit(solution)/shard_map/ppermute | solution.py:902
  30.3 37.4 %collective-permute-start.8 = (bf16[108,16,128]{2,1,0:T(8,128)(2,1)S(1)}, bf16[108,16,128]{2,1,0:T(8,128)(2,1)S(1)}, u32[]{:S(2)}, u32[]{:S(2)}) collective-permute-start(bf16[108,16,128]{2,1,0:T(8,128)(2,1)S(1)} %bitcast.119), channel_id=1, source_target_pairs={{0,6},{1,7},{2,4},{3,5},{4,2},{5,3},{6,0},{7,1},{8,14},{9,15},{10,... | collective-permute-start | bytes 1327112 | tf_op jit(solution)/shard_map/ppermute | solution.py:902
  39.6 28.4 %collective-permute-start.4 = (bf16[128,16,128]{2,1,0:T(8,128)(2,1)S(1)}, bf16[128,16,128]{2,1,0:T(8,128)(2,1)S(1)}, u32[]{:S(2)}, u32[]{:S(2)}) collective-permute-start(bf16[128,16,128]{2,1,0:T(8,128)(2,1)S(1)} %pad_maximum_fusion.7), channel_id=1, source_target_pairs={{0,16},{1,17},{2,18},{3,19},{4,20},{5,21},{6,22},{7,23},{8,24},{9,... | collective-permute-start | bytes 1572872 | tf_op jit(solution)/shard_map/ppermute | solution.py:902
  39.7 28.4 %collective-permute-start.9 = (bf16[108,16,128]{2,1,0:T(8,128)(2,1)S(1)}, bf16[108,16,128]{2,1,0:T(8,128)(2,1)S(1)}, u32[]{:S(2)}, u32[]{:S(2)}) collective-permute-start(bf16[108,16,128]{2,1,0:T(8,128)(2,1)S(1)} %pad_maximum_fusion.9), channel_id=1, source_target_pairs={{0,8},{1,9},{2,10},{3,11},{4,12},{5,13},{6,14},{7,15},{8,0},{9,1},... | collective-permute-start | bytes 1327112 | tf_op jit(solution)/shard_map/ppermute | solution.py:902
  72.9 24.9 %collective-permute-start.15 = (bf16[2048,128]{1,0:T(8,128)(2,1)S(1)}, bf16[2048,128]{1,0:T(8,128)(2,1)S(1)}, u32[]{:S(2)}, u32[]{:S(2)}) collective-permute-start(bf16[2048,128]{1,0:T(8,128)(2,1)S(1)} %pad_maximum_fusion.8), channel_id=1, source_target_pairs={{0,4},{1,5},{2,6},{3,7},{4,0},{5,1},{6,2},{7,3},{8,12},{9,13},{10,... | collective-permute-start | bytes 1572872 | tf_op jit(solution)/shard_map/ppermute | solution.py:902
  75.2 45.2 %collective-permute-start.16 = (bf16[2048,128]{1,0:T(8,128)(2,1)S(1)}, bf16[2048,128]{1,0:T(8,128)(2,1)S(1)}, u32[]{:S(2)}, u32[]{:S(2)}) collective-permute-start(bf16[2048,128]{1,0:T(8,128)(2,1)S(1)} %pad_maximum_fusion.8), channel_id=1, source_target_pairs={{0,6},{1,7},{2,4},{3,5},{4,2},{5,3},{6,0},{7,1},{8,14},{9,15},{10,... | collective-permute-start | bytes 1572872 | tf_op jit(solution)/shard_map/ppermute | solution.py:902
  86.3 37.2 %collective-permute-start.13 = (bf16[324,16,128]{2,1,0:T(8,128)(2,1)S(1)}, bf16[324,16,128]{2,1,0:T(8,128)(2,1)}, u32[]{:S(2)}, u32[]{:S(2)}) collective-permute-start(bf16[324,16,128]{2,1,0:T(8,128)(2,1)S(1)} %pad_maximum_fusion.1), channel_id=1, source_target_pairs={{0,8},{1,9},{2,10},{3,11},{4,12},{5,13},{6,14},{7,15},{8,0},{9,1},... | collective-permute-start | bytes 3981320 | tf_op jit(solution)/shard_map/ppermute | solution.py:902
  86.5 36.9 %collective-permute-start.11 = (bf16[324,16,128]{2,1,0:T(8,128)(2,1)S(1)}, bf16[324,16,128]{2,1,0:T(8,128)(2,1)}, u32[]{:S(2)}, u32[]{:S(2)}) collective-permute-start(bf16[324,16,128]{2,1,0:T(8,128)(2,1)S(1)} %pad_maximum_fusion), channel_id=1, source_target_pairs={{0,16},{1,17},{2,18},{3,19},{4,20},{5,21},{6,22},{7,23},{8,24},{9,... | collective-permute-start | bytes 3981320 | tf_op jit(solution)/shard_map/ppermute | solution.py:902
  153.7 40.3 %collective-permute-start.23 = (bf16[432,16,128]{2,1,0:T(8,128)(2,1)}, bf16[432,16,128]{2,1,0:T(8,128)(2,1)}, u32[]{:S(2)}, u32[]{:S(2)}) collective-permute-start(bf16[432,16,128]{2,1,0:T(8,128)(2,1)} %constant_dynamic-update-slice_fusion.12), channel_id=1, source_target_pairs={{0,8},{1,9},{2,10},{3,11},{4,12},{5,13},{6,14},{7,15},{8,0},{9,1},... | collective-permute-start | bytes 5308424 | tf_op jit(solution)/shard_map/ppermute | solution.py:902
  154.9 39.1 %collective-permute-start.26 = (bf16[432,16,128]{2,1,0:T(8,128)(2,1)S(1)}, bf16[432,16,128]{2,1,0:T(8,128)(2,1)}, u32[]{:S(2)}, u32[]{:S(2)}) collective-permute-start(bf16[432,16,128]{2,1,0:T(8,128)(2,1)S(1)} %get-tuple-element.251.refs_4_), channel_id=1, source_target_pairs={{0,1},{1,0},{2,3},{3,2},{4,5},{5,4},{6,7},{7,6},{8,9},{9,8},{10,11... | collective-permute-start | bytes 5308424 | tf_op jit(solution)/shard_map/ppermute | solution.py:902
  156.4 40.3 %collective-permute-start.22 = (bf16[432,16,128]{2,1,0:T(8,128)(2,1)S(1)}, bf16[432,16,128]{2,1,0:T(8,128)(2,1)}, u32[]{:S(2)}, u32[]{:S(2)}) collective-permute-start(bf16[432,16,128]{2,1,0:T(8,128)(2,1)S(1)} %constant_dynamic-update-slice_fusion.10), channel_id=1, source_target_pairs={{0,16},{1,17},{2,18},{3,19},{4,20},{5,21},{6,22},{7,23},{8,24},{9,... | collective-permute-start | bytes 5308424 | tf_op jit(solution)/shard_map/ppermute | solution.py:902
  156.4 37.6 %collective-permute-start.24 = (bf16[216,16,128]{2,1,0:T(8,128)(2,1)}, bf16[216,16,128]{2,1,0:T(8,128)(2,1)}, u32[]{:S(2)}, u32[]{:S(2)}) collective-permute-start(bf16[216,16,128]{2,1,0:T(8,128)(2,1)} %collective-permute-done.17.refs_0_), channel_id=1, source_target_pairs={{0,1},{1,0},{2,3},{3,2},{4,5},{5,4},{6,7},{7,6},{8,9},{9,8},{10,11... | collective-permute-start | bytes 2654216 | tf_op jit(solution)/shard_map/ppermute | solution.py:902
  156.6 37.3 %collective-permute-start.25 = (bf16[216,16,128]{2,1,0:T(8,128)(2,1)}, bf16[216,16,128]{2,1,0:T(8,128)(2,1)}, u32[]{:S(2)}, u32[]{:S(2)}) collective-permute-start(bf16[216,16,128]{2,1,0:T(8,128)(2,1)} %collective-permute-done.18.refs_1_), channel_id=1, source_target_pairs={{0,1},{1,0},{2,3},{3,2},{4,5},{5,4},{6,7},{7,6},{8,9},{9,8},{10,11... | collective-permute-start | bytes 2654216 | tf_op jit(solution)/shard_map/ppermute | solution.py:902
  292.8 40.0 %collective-permute-start.32 = (bf16[432,16,128]{2,1,0:T(8,128)(2,1)}, bf16[432,16,128]{2,1,0:T(8,128)(2,1)S(1)}, u32[]{:S(2)}, u32[]{:S(2)}) collective-permute-start(bf16[432,16,128]{2,1,0:T(8,128)(2,1)} %get-tuple-element.289), channel_id=1, source_target_pairs={{0,16},{1,17},{2,18},{3,19},{4,20},{5,21},{6,22},{7,23},{8,24},{9,... | collective-permute-start | bytes 5308424 | tf_op jit(solution)/shard_map/ppermute | solution.py:902
  292.8 40.0 %collective-permute-start.31 = (bf16[432,16,128]{2,1,0:T(8,128)(2,1)}, bf16[432,16,128]{2,1,0:T(8,128)(2,1)S(1)}, u32[]{:S(2)}, u32[]{:S(2)}) collective-permute-start(bf16[432,16,128]{2,1,0:T(8,128)(2,1)} %get-tuple-element.284), channel_id=1, source_target_pairs={{0,8},{1,9},{2,10},{3,11},{4,12},{5,13},{6,14},{7,15},{8,0},{9,1},... | collective-permute-start | bytes 5308424 | tf_op jit(solution)/shard_map/ppermute | solution.py:902
  347.3 46.3 %collective-permute-start.36 = (bf16[432,16,128]{2,1,0:T(8,128)(2,1)}, bf16[432,16,128]{2,1,0:T(8,128)(2,1)}, u32[]{:S(2)}, u32[]{:S(2)}) collective-permute-start(bf16[432,16,128]{2,1,0:T(8,128)(2,1)} %get-tuple-element.333), channel_id=1, source_target_pairs={{0,16},{1,17},{2,18},{3,19},{4,20},{5,21},{6,22},{7,23},{8,24},{9,... | collective-permute-start | bytes 5308424 | tf_op jit(solution)/shard_map/ppermute | solution.py:902
  348.7 44.8 %collective-permute-start.35 = (bf16[432,16,128]{2,1,0:T(8,128)(2,1)}, bf16[432,16,128]{2,1,0:T(8,128)(2,1)}, u32[]{:S(2)}, u32[]{:S(2)}) collective-permute-start(bf16[432,16,128]{2,1,0:T(8,128)(2,1)} %get-tuple-element.325), channel_id=1, source_target_pairs={{0,8},{1,9},{2,10},{3,11},{4,12},{5,13},{6,14},{7,15},{8,0},{9,1},... | collective-permute-start | bytes 5308424 | tf_op jit(solution)/shard_map/ppermute | solution.py:902
  358.1 31.9 %collective-permute-start.41 = (bf16[108,16,128]{2,1,0:T(8,128)(2,1)}, bf16[108,16,128]{2,1,0:T(8,128)(2,1)}, u32[]{:S(2)}, u32[]{:S(2)}) collective-permute-start(bf16[108,16,128]{2,1,0:T(8,128)(2,1)} %pad_maximum_fusion.13), channel_id=1, source_target_pairs={{0,6},{1,7},{2,4},{3,5},{4,2},{5,3},{6,0},{7,1},{8,14},{9,15},{10,... | collective-permute-start | bytes 1327112 | tf_op jit(solution)/shard_map/ppermute | solution.py:902
  360.1 29.9 %collective-permute-start.40 = (bf16[108,16,128]{2,1,0:T(8,128)(2,1)}, bf16[108,16,128]{2,1,0:T(8,128)(2,1)}, u32[]{:S(2)}, u32[]{:S(2)}) collective-permute-start(bf16[108,16,128]{2,1,0:T(8,128)(2,1)} %pad_maximum_fusion.12), channel_id=1, source_target_pairs={{0,4},{1,5},{2,6},{3,7},{4,0},{5,1},{6,2},{7,3},{8,12},{9,13},{10,... | collective-permute-start | bytes 1327112 | tf_op jit(solution)/shard_map/ppermute | solution.py:902
  361.0 29.1 %collective-permute-start.39 = (bf16[108,16,128]{2,1,0:T(8,128)(2,1)}, bf16[108,16,128]{2,1,0:T(8,128)(2,1)}, u32[]{:S(2)}, u32[]{:S(2)}) collective-permute-start(bf16[108,16,128]{2,1,0:T(8,128)(2,1)} %pad_maximum_fusion.11), channel_id=1, source_target_pairs={{0,2},{1,3},{2,0},{3,1},{4,6},{5,7},{6,4},{7,5},{8,10},{9,11},{10,... | collective-permute-start | bytes 1327112 | tf_op jit(solution)/shard_map/ppermute | solution.py:902
  418.8 46.0 %collective-permute-start.49 = (bf16[108,16,128]{2,1,0:T(8,128)(2,1)S(1)}, bf16[108,16,128]{2,1,0:T(8,128)(2,1)S(1)}, u32[]{:S(2)}, u32[]{:S(2)}) collective-permute-start(bf16[108,16,128]{2,1,0:T(8,128)(2,1)S(1)} %pad_maximum_fusion.17), channel_id=1, source_target_pairs={{0,6},{1,7},{2,4},{3,5},{4,2},{5,3},{6,0},{7,1},{8,14},{9,15},{10,... | collective-permute-start | bytes 1327112 | tf_op jit(solution)/shard_map/ppermute | solution.py:902
  420.1 44.7 %collective-permute-start.48 = (bf16[108,16,128]{2,1,0:T(8,128)(2,1)S(1)}, bf16[108,16,128]{2,1,0:T(8,128)(2,1)S(1)}, u32[]{:S(2)}, u32[]{:S(2)}) collective-permute-start(bf16[108,16,128]{2,1,0:T(8,128)(2,1)S(1)} %pad_maximum_fusion.16), channel_id=1, source_target_pairs={{0,4},{1,5},{2,6},{3,7},{4,0},{5,1},{6,2},{7,3},{8,12},{9,13},{10,... | collective-permute-start | bytes 1327112 | tf_op jit(solution)/shard_map/ppermute | solution.py:902
  423.9 40.9 %collective-permute-start.47 = (bf16[108,16,128]{2,1,0:T(8,128)(2,1)S(1)}, bf16[108,16,128]{2,1,0:T(8,128)(2,1)S(1)}, u32[]{:S(2)}, u32[]{:S(2)}) collective-permute-start(bf16[108,16,128]{2,1,0:T(8,128)(2,1)S(1)} %pad_maximum_fusion.15), channel_id=1, source_target_pairs={{0,2},{1,3},{2,0},{3,1},{4,6},{5,7},{6,4},{7,5},{8,10},{9,11},{10,... | collective-permute-start | bytes 1327112 | tf_op jit(solution)/shard_map/ppermute | solution.py:902
  428.2 32.8 %collective-permute-start.52 = (bf16[384,128]{1,0:T(8,128)(2,1)S(1)}, bf16[384,128]{1,0:T(8,128)(2,1)S(1)}, u32[]{:S(2)}, u32[]{:S(2)}) collective-permute-start(bf16[384,128]{1,0:T(8,128)(2,1)S(1)} %bitcast.124), channel_id=1, source_target_pairs={{0,1},{1,2},{2,3},{3,4},{4,5},{5,6},{6,7},{7,8},{8,9},{9,10},{10,1... | collective-permute-start | bytes 294920 | tf_op jit(solution)/shard_map/ppermute | solution.py:116
  (51 other events, 538.7 us)
where the time goes:
time: 486 us; the launch traced here: 478 us
  Pallas kernels  183 us (38%)
  waiting for transfers between devices  141 us (29%)
  starting transfers between devices  63.2 us (13%)
  other arithmetic  39.4 us (8%)
  local copies, waits for them, and re-layouts  36.1 us (7%)
  matrix products  13.4 us (3%)
    ppermute x50, waiting for transfers between devices, exchange(): return lax.ppermute(block, AXES, perm)  119 us
    ppermute x50, starting transfers between devices, exchange(): return lax.ppermute(block, AXES, perm)  42.4 us
    pallas_call x2, Pallas kernels, project(): pl.pallas_call(functools.partial(project_kernel, places, slots), grid_spe...  28.4 us
    pallas_call x2, Pallas kernels, mlp(): pl.pallas_call(mlp_kernel, grid=(1,), in_specs=[whole_spec(array.shape) f...  26.5 us
    pallas_call x2, Pallas kernels, mlp_back(): pl.pallas_call(mlp_back_kernel, grid=(1,), in_specs=[whole_spec(array.sha...  26.4 us
    pallas_call x2, Pallas kernels, weight_back(): pl.pallas_call(functools.partial(weight_back_kernel, places, stepwise), g...  25.7 us
    pallas_call x2, Pallas kernels, attention_back(): pl.pallas_call(functools.partial(attention_back_kernel, pairs), grid=(ste...  21.6 us
    ppermute x3, waiting for transfers between devices, halo(): pieces.append(lax.ppermute(block[..., :take, :], AXES, perm))  21.4 us
  transfers between devices with their start and end apart: 56, of which 25 were waited for; matrix products, arithmetic and copies ran while one was open for 13% of the time, Pallas kernels for 23%

commit v1 on v0

--- a/solution.py
+++ b/solution.py
@@ -1063,9 +1063,12 @@
         normed, qkv, tiles = project(self.places, self.position, parts, hidden, self.vectors)
         self.saved = dict(hidden=hidden, normed=normed, qkv=qkv, tiles=tiles)
 
-    def forward(self):
+    def attend(self):
         saved = self.saved
         saved["attended"], saved["weights"] = attention(self.counts, saved["qkv"], self.bias)
+
+    def finish(self):
+        saved = self.saved
         names = ("branch", "middle", "normed2", "activ", "slope", "mlp_out")
         result, *kept = mlp(saved["attended"], saved["hidden"], self.vectors, saved["tiles"])
         saved.update(zip(names, kept))
@@ -1132,19 +1135,20 @@
         far_second, early, group, small_rows, vectors = tie(far_second, early, group, small_rows, vectors)
         first = fetch_plane(places, group, 0)
         parts = fetch_core(places, early) + fetch_core(places, list_core(places, [far_second]))
-        entries = table_entries(small_rows)
         first_layer = Layer(places, position, counts, vectors[0])
+        parts, group = tie(parts, group)
+        second_early = fetch_plane(places, group, 1)
+        first_layer.project(hidden, parts)
+        entries, first_layer.saved = tie(table_entries(small_rows), first_layer.saved)
         first_layer.bias, second_bias = bias_of(entries[0]), bias_of(entries[1])
-        first, group, parts, first_layer.bias, second_bias = tie(first, group, parts, first_layer.bias, second_bias)
-        second_group = merge(group, first)
-        second = fetch_plane(places, second_group, 1)
-        parts, _ = tie(parts, second_group)
-        next_parts = fetch_core(places, list_core(places, [first]))
-        first_layer.project(hidden, parts)
-        result = first_layer.forward()
+        first, second_early, first_layer.bias, second_bias = tie(first, second_early, first_layer.bias, second_bias)
+        second = fetch_plane(places, first, 1)
+        next_parts = fetch_core(places, list_core(places, [first, second_early]))
+        first_layer.attend()
+        result = first_layer.finish()
         next_parts, result = tie(next_parts, result)
         next_parts += fetch_core(places, gather_core(places, [group]))
-        second, next_parts, result, second_bias = tie(second, next_parts, result, second_bias)
+        second, next_parts, result = tie(second, next_parts, result)
         next_parts += fetch_core(places, list_core(places, [second]))
     else:
         vectors = small_rows.astype(jnp.float32)
@@ -1157,11 +1161,13 @@
         first_layer = Layer(places, position, counts, vectors[0])
         first_layer.project(hidden, parts)
         first_layer.bias = bias_of(entries[0])
-        result = first_layer.forward()
+        first_layer.attend()
+        result = first_layer.finish()
     second_layer = Layer(places, position, counts, vectors[1])
     second_layer.bias = second_bias
     second_layer.project(result, next_parts)
-    result = second_layer.forward()
+    second_layer.attend()
+    result = second_layer.finish()
     output = cut_rows(result)
 
     next_passed = second_layer.back_mlp(grad_output)

time: 486 us -> 482 us (level)
  local copies, waits for them, and re-layouts: 36.1 us -> 29.5 us
    concatenate x4 -> x2, local copies, waits for them, and re-layouts: 6.32 us -> 1.17 us  [join(): return jnp.concatenate(blocks, axis=0) if len(blocks) > 1 else blocks[0]]
    ppermute x50 -> x54, starting transfers between devices: 42.4 us -> 45.2 us  [exchange(): return lax.ppermute(block, AXES, perm)]
    ppermute x50 -> x54, waiting for transfers between devices: 119 us -> 117 us  [exchange(): return lax.ppermute(block, AXES, perm)]
    unnamed x54 -> x63, local copies, waits for them, and re-layouts: 12.9 us -> 11.4 us
  transfers between devices with their start and end apart: 56 -> 60, of which waited for: 25 -> 28; matrix products, arithmetic and copies ran while one was open for 13% -> 13% of each run, Pallas kernels for 23% -> 23%
where the time goes in v1:
time: 482 us; the launch traced here: 474 us
  Pallas kernels  183 us (38%)
  waiting for transfers between devices  140 us (29%)
  starting transfers between devices  66.6 us (14%)
  other arithmetic  39.4 us (8%)
  local copies, waits for them, and re-layouts  29.5 us (6%)
  matrix products  13.4 us (3%)
    ppermute x54, waiting for transfers between devices, exchange(): return lax.ppermute(block, AXES, perm)  117 us
    ppermute x54, starting transfers between devices, exchange(): return lax.ppermute(block, AXES, perm)  45.2 us
    pallas_call x2, Pallas kernels, project(): pl.pallas_call(functools.partial(project_kernel, places, slots), grid_spe...  28.4 us
    pallas_call x2, Pallas kernels, mlp(): pl.pallas_call(mlp_kernel, grid=(1,), in_specs=[whole_spec(array.shape) f...  26.5 us
    pallas_call x2, Pallas kernels, mlp_back(): pl.pallas_call(mlp_back_kernel, grid=(1,), in_specs=[whole_spec(array.sha...  26.4 us
    pallas_call x2, Pallas kernels, weight_back(): pl.pallas_call(functools.partial(weight_back_kernel, places, stepwise), g...  25.7 us
    ppermute x3, waiting for transfers between devices, halo(): pieces.append(lax.ppermute(block[..., :take, :], AXES, perm))  22.4 us
    pallas_call x2, Pallas kernels, attention_back(): pl.pallas_call(functools.partial(attention_back_kernel, pairs), grid=(ste...  21.7 us
  transfers between devices with their start and end apart: 60, of which 28 were waited for; matrix products, arithmetic and copies ran while one was open for 13% of the time, Pallas kernels for 23%

profile of v1, /device:TPU:11, one launch (start us, length us, event | category | flops | bytes accessed | tf_op | source)
XLA Modules:
  0.0 473.7 jit_solution(9207659908783317265)
XLA Ops:
  41.3 18.1 %collective-permute-done.7 = bf16[108,16,128]{2,1,0:T(8,128)(2,1)S(1)} collective-permute-done((bf16[108,16,128]{2,1,0:T(8,128)(2,1)S(1)}, bf16[108,16,128]{2,1,0:T(8,128)(2,1)S(1)}, u32[]{:S(2)}, u32[]{:S(2)}) %collective-permute-start.7) | collective-permute-done | bytes 442400 | tf_op jit(solution)/shard_map/ppermute | solution.py:902
  59.4 8.4 %collective-permute-done.8 = bf16[108,16,128]{2,1,0:T(8,128)(2,1)S(1)} collective-permute-done((bf16[108,16,128]{2,1,0:T(8,128)(2,1)S(1)}, bf16[108,16,128]{2,1,0:T(8,128)(2,1)S(1)}, u32[]{:S(2)}, u32[]{:S(2)}) %collective-permute-start.8) | collective-permute-done | bytes 442400 | tf_op jit(solution)/shard_map/ppermute | solution.py:902
  77.5 8.7 %collective-permute-done.12 = bf16[162,16,128]{2,1,0:T(8,128)(2,1)S(1)} collective-permute-done((bf16[162,16,128]{2,1,0:T(8,128)(2,1)S(1)}, bf16[162,16,128]{2,1,0:T(8,128)(2,1)S(1)}, u32[]{:S(2)}, u32[]{:S(2)}) %collective-permute-start.12) | collective-permute-done | bytes 663584 | tf_op jit(solution)/shard_map/ppermute | solution.py:902
  88.1 6.2 %collective-permute-done.14 = bf16[2048,128]{1,0:T(8,128)(2,1)S(1)} collective-permute-done((bf16[2048,128]{1,0:T(8,128)(2,1)S(1)}, bf16[2048,128]{1,0:T(8,128)(2,1)S(1)}, u32[]{:S(2)}, u32[]{:S(2)}) %collective-permute-start.14) | collective-permute-done | bytes 524320 | tf_op jit(solution)/shard_map/ppermute | solution.py:902
  97.8 22.7 %collective-permute-done.16 = bf16[2048,128]{1,0:T(8,128)(2,1)S(1)} collective-permute-done((bf16[2048,128]{1,0:T(8,128)(2,1)S(1)}, bf16[2048,128]{1,0:T(8,128)(2,1)S(1)}, u32[]{:S(2)}, u32[]{:S(2)}) %collective-permute-start.16) | collective-permute-done | bytes 524320 | tf_op jit(solution)/shard_map/ppermute | solution.py:902
  126.4 10.0 %collective-permute-done.20.refs_4_ = bf16[324,16,128]{2,1,0:T(8,128)(2,1)} collective-permute-done((bf16[324,16,128]{2,1,0:T(8,128)(2,1)}, bf16[324,16,128]{2,1,0:T(8,128)(2,1)}, u32[]{:S(2)}, u32[]{:S(2)}) %collective-permute-start.20) | collective-permute-done | bytes 1327136 | tf_op jit(solution)/shard_map/ppermute | solution.py:902
  140.7 14.2 %project.2 = (bf16[416,768]{1,0:T(8,128)(2,1)}, bf16[416,2304]{1,0:T(8,128)(2,1)}, bf16[3456,16,128]{2,1,0:T(8,128)(2,1)}) custom-call(s32[4]{0:T(128)} %pad_add_fusion.at_ref, bf16[1080,16,128]{2,1,0:T(8,128)(2,1)} %constant_dynamic-update-slice_fusion.refs_0_, bf16[1080,16,128]{2,1,0:T(8,128)(2,1)} %collective-permute-done.19.refs_1_, ...), custom_call_target="tpu_custom_call" | custom-call | tf_op jit(solution)/shard_map/project/pallas_call | solution.py:562
  172.5 7.4 %attention.2 = (bf16[416,768]{1,0:T(8,128)(2,1)}, bf16[2,12,208,208]{3,2,1,0:T(8,128)(2,1)}) custom-call(s32[2]{0:T(128)} %counts_ref.3, bf16[416,2304]{1,0:T(8,128)(2,1)} %get-tuple-element.244.query_ref.key_ref.value_ref, bf16[416,2304]{1,0:T(8,128)(2,1)} %get-tuple-element.244.query_ref.key_ref.value_ref, ...), custom_call_target="tpu_custom_call" | custom-call | tf_op jit(solution)/shard_map/attention/pallas_call | solution.py:413
  179.9 13.3 %mlp.2 = (f32[416,768]{1,0:T(8,128)}, bf16[416,768]{1,0:T(8,128)(2,1)}, f32[416,768]{1,0:T(8,128)}, bf16[416,768]{1,0:T(8,128)(2,1)}, bf16[416,3072]{1,0:T(8,128...) custom-call(bf16[416,768]{1,0:T(8,128)(2,1)} %get-tuple-element.246.attended_ref.refs_2_, ...), custom_call_target="tpu_custom_call" | custom-call | tf_op jit(solution)/shard_map/mlp/pallas_call | solution.py:672
  198.5 14.2 %project.3 = (bf16[416,768]{1,0:T(8,128)(2,1)}, bf16[416,2304]{1,0:T(8,128)(2,1)}, bf16[3456,16,128]{2,1,0:T(8,128)(2,1)}) custom-call(s32[4]{0:T(128)} %pad_add_fusion.at_ref, bf16[216,16,128]{2,1,0:T(8,128)(2,1)} %collective-permute-done.17.refs_0_, bf16[216,16,128]{2,1,0:T(8,128)(2,1)} %collective-permute-done.18.refs_1_, ...), custom_call_target="tpu_custom_call" | custom-call | tf_op jit(solution)/shard_map/project/pallas_call | solution.py:562
  212.7 7.8 %attention.3 = (bf16[416,768]{1,0:T(8,128)(2,1)}, bf16[2,12,208,208]{3,2,1,0:T(8,128)(2,1)}) custom-call(s32[2]{0:T(128)} %counts_ref.3, bf16[416,2304]{1,0:T(8,128)(2,1)} %get-tuple-element.273.query_ref.key_ref.value_ref, bf16[416,2304]{1,0:T(8,128)(2,1)} %get-tuple-element.273.query_ref.key_ref.value_ref, ...), custom_call_target="tpu_custom_call" | custom-call | tf_op jit(solution)/shard_map/attention/pallas_call | solution.py:413
  220.5 13.2 %mlp.3 = (f32[416,768]{1,0:T(8,128)}, bf16[416,768]{1,0:T(8,128)(2,1)}, f32[416,768]{1,0:T(8,128)}, bf16[416,768]{1,0:T(8,128)(2,1)}, bf16[416,3072]{1,0:T(8,128...) custom-call(bf16[416,768]{1,0:T(8,128)(2,1)} %get-tuple-element.276.attended_ref.refs_2_, ...), custom_call_target="tpu_custom_call" | custom-call | tf_op jit(solution)/shard_map/mlp/pallas_call | solution.py:672
  233.7 13.3 %mlp_back.2 = (f32[416,768]{1,0:T(8,128)}, bf16[416,768]{1,0:T(8,128)(2,1)}, bf16[416,768]{1,0:T(8,128)(2,1)}, bf16[416,3072]{1,0:T(8,128)(2,1)}, bf16[416,768]{1,0:T(8,128)(2,1)}, /*index=5*/f32[64,128]{1,0:T(8,128)}) custom-call(f32[416,768]{1,0:T(8,128)} %bitcast.86, bf16[416,768]{1,0:T(8,128)(2,1)} %get-tuple-element.278.branch_ref, ...), custom_call_target="tpu_custom_call" | custom-call | tf_op jit(solution)/shard_map/mlp_back/pallas_call | solution.py:744
  247.0 10.8 %attention_back.2 = (bf16[3,416,768]{2,1,0:T(8,128)(2,1)}, f32[12,208,208]{2,1,0:T(8,128)}) custom-call(bf16[416,2304]{1,0:T(8,128)(2,1)} %get-tuple-element.273.query_ref.key_ref.value_ref, bf16[416,2304]{1,0:T(8,128)(2,1)} %get-tuple-element.273.query_ref.key_ref.value_ref, bf16[416,2304]{1,0:T(8,128)(2,1)} %get-tuple-element.273.query_ref.key_ref.value_ref, ...), custom_call_target="tpu_custom_call" | custom-call | tf_op jit(solution)/shard_map/attention_back/pallas_call | solution.py:433
  257.8 12.8 %weight_back.2 = (bf16[864,16,128]{2,1,0:T(8,128)(2,1)}, bf16[864,16,128]{2,1,0:T(8,128)(2,1)}, bf16[864,16,128]{2,1,0:T(8,128)(2,1)}, bf16[864,16,128]{2,1,0:T(8,128)(2,1)}) custom-call(s32[4]{0:T(128)} %pad_add_fusion.at_ref, bf16[416,768]{1,0:T(8,128)(2,1)} %get-tuple-element.272.refs_0_, bf16[3,416,768]{2,1,0:T(8,128)(2,1)} %get-tuple-element.284.refs_1_.project_ref, ...), custom_call_target="tpu_custom_call" | custom-call | tf_op jit(solution)/shard_map/weight_back/pallas_call | solution.py:827
  271.3 6.7 %input_back.2 = (f32[416,768]{1,0:T(8,128)}, f32[24,128]{1,0:T(8,128)}) custom-call(bf16[3,416,768]{2,1,0:T(8,128)(2,1)} %get-tuple-element.284.refs_1_.project_ref, f32[416,768]{1,0:T(8,128)} %get-tuple-element.294.grad_middle_ref, f32[416,768]{1,0:T(8,128)} %get-tuple-element.271.refs_14_.hidden_ref, f32[160,128]{1,0:T(8,128)} %get-tuple-element.446.refs_15_.vectors_ref, ...), custom_call_target="tpu_custom_call" | custom-call | tf_op jit(solution)/shard_map/input_back/pallas_call | solution.py:867
  288.2 13.1 %mlp_back.3 = (f32[416,768]{1,0:T(8,128)}, bf16[416,768]{1,0:T(8,128)(2,1)}, bf16[416,768]{1,0:T(8,128)(2,1)}, bf16[416,3072]{1,0:T(8,128)(2,1)}, bf16[416,768]{1,0:T(8,128)(2,1)}, /*index=5*/f32[64,128]{1,0:T(8,128)}) custom-call(f32[416,768]{1,0:T(8,128)} %get-tuple-element.307.grad_ref, bf16[416,768]{1,0:T(8,128)(2,1)} %get-tuple-element.308.branch_ref, ...), custom_call_target="tpu_custom_call" | custom-call | tf_op jit(solution)/shard_map/mlp_back/pallas_call | solution.py:744
  301.3 10.9 %attention_back.3 = (bf16[3,416,768]{2,1,0:T(8,128)(2,1)}, f32[12,208,208]{2,1,0:T(8,128)}) custom-call(bf16[416,2304]{1,0:T(8,128)(2,1)} %get-tuple-element.244.query_ref.key_ref.value_ref, bf16[416,2304]{1,0:T(8,128)(2,1)} %get-tuple-element.244.query_ref.key_ref.value_ref, bf16[416,2304]{1,0:T(8,128)(2,1)} %get-tuple-element.244.query_ref.key_ref.value_ref, ...), custom_call_target="tpu_custom_call" | custom-call | tf_op jit(solution)/shard_map/attention_back/pallas_call | solution.py:433
  312.1 12.9 %weight_back.3 = (bf16[864,16,128]{2,1,0:T(8,128)(2,1)}, bf16[864,16,128]{2,1,0:T(8,128)(2,1)}, bf16[864,16,128]{2,1,0:T(8,128)(2,1)}, bf16[864,16,128]{2,1,0:T(8,128)(2,1)}) custom-call(s32[4]{0:T(128)} %pad_add_fusion.at_ref, bf16[416,768]{1,0:T(8,128)(2,1)} %get-tuple-element.306.refs_0_, bf16[3,416,768]{2,1,0:T(8,128)(2,1)} %get-tuple-element.362.refs_1_.project_ref, ...), custom_call_target="tpu_custom_call" | custom-call | tf_op jit(solution)/shard_map/weight_back/pallas_call | solution.py:827
  343.4 6.2 %collective-permute-done.42 = bf16[216,16,128]{2,1,0:T(8,128)(2,1)S(1)} collective-permute-done((bf16[216,16,128]{2,1,0:T(8,128)(2,1)S(1)}, bf16[216,16,128]{2,1,0:T(8,128)(2,1)S(1)}, u32[]{:S(2)}, u32[]{:S(2)}) %collective-permute-start.42) | collective-permute-done | bytes 884768 | tf_op jit(solution)/shard_map/ppermute | solution.py:902
  357.7 14.9 %table_back.1 = f32[32,768]{1,0:T(8,128)} custom-call(f32[12,208,208]{2,1,0:T(8,128)} %get-tuple-element.368.first_ref, f32[12,208,208]{2,1,0:T(8,128)} %get-tuple-element.369.second_ref), custom_call_target="tpu_custom_call" | custom-call | tf_op jit(solution)/shard_map/table_back/pallas_call | solution.py:319
  377.9 6.6 %input_back.3 = (f32[416,768]{1,0:T(8,128)}, f32[24,128]{1,0:T(8,128)}) custom-call(bf16[3,416,768]{2,1,0:T(8,128)(2,1)} %get-tuple-element.362.refs_1_.project_ref, f32[416,768]{1,0:T(8,128)} %get-tuple-element.363.grad_middle_ref, f32[416,768]{1,0:T(8,128)} %bitcast.85, f32[160,128]{1,0:T(8,128)} %get-tuple-element.447.refs_7_.vectors_ref, ...), custom_call_target="tpu_custom_call" | custom-call | tf_op jit(solution)/shard_map/input_back/pallas_call | solution.py:867
  422.6 8.0 %collective-permute-start.56 = (bf16[384,128]{1,0:T(8,128)(2,1)S(1)}, bf16[384,128]{1,0:T(8,128)(2,1)S(1)}, u32[]{:S(2)}, u32[]{:S(2)}) collective-permute-start(bf16[384,128]{1,0:T(8,128)(2,1)S(1)} %bitcast.124), channel_id=1, source_target_pairs={{0,1},{1,2},{2,3},{3,4},{4,5},{5,6},{6,7},{7,8},{8,9},{9,10},{10,1... | collective-permute-start | bytes 294920 | tf_op jit(solution)/shard_map/ppermute | solution.py:116
  435.2 21.1 %collective-permute-done.57 = bf16[288,128]{1,0:T(8,128)(2,1)S(1)} collective-permute-done((bf16[288,128]{1,0:T(8,128)(2,1)S(1)}, bf16[288,128]{1,0:T(8,128)(2,1)S(1)}, u32[]{:S(2)}, u32[]{:S(2)}) %collective-permute-start.57) | collective-permute-done | bytes 73760 | tf_op jit(solution)/shard_map/ppermute | solution.py:120
  (282 shorter events, 190.2 us)
Async XLA Ops:
  24.7 34.7 %collective-permute-start.7 = (bf16[108,16,128]{2,1,0:T(8,128)(2,1)S(1)}, bf16[108,16,128]{2,1,0:T(8,128)(2,1)S(1)}, u32[]{:S(2)}, u32[]{:S(2)}) collective-permute-start(bf16[108,16,128]{2,1,0:T(8,128)(2,1)S(1)} %bitcast.118), channel_id=1, source_target_pairs={{0,4},{1,5},{2,6},{3,7},{4,0},{5,1},{6,2},{7,3},{8,12},{9,13},{10,... | collective-permute-start | bytes 1327112 | tf_op jit(solution)/shard_map/ppermute | solution.py:902
  30.3 37.4 %collective-permute-start.8 = (bf16[108,16,128]{2,1,0:T(8,128)(2,1)S(1)}, bf16[108,16,128]{2,1,0:T(8,128)(2,1)S(1)}, u32[]{:S(2)}, u32[]{:S(2)}) collective-permute-start(bf16[108,16,128]{2,1,0:T(8,128)(2,1)S(1)} %bitcast.119), channel_id=1, source_target_pairs={{0,6},{1,7},{2,4},{3,5},{4,2},{5,3},{6,0},{7,1},{8,14},{9,15},{10,... | collective-permute-start | bytes 1327112 | tf_op jit(solution)/shard_map/ppermute | solution.py:902
  39.6 28.4 %collective-permute-start.4 = (bf16[128,16,128]{2,1,0:T(8,128)(2,1)S(1)}, bf16[128,16,128]{2,1,0:T(8,128)(2,1)S(1)}, u32[]{:S(2)}, u32[]{:S(2)}) collective-permute-start(bf16[128,16,128]{2,1,0:T(8,128)(2,1)S(1)} %pad_maximum_fusion.7), channel_id=1, source_target_pairs={{0,16},{1,17},{2,18},{3,19},{4,20},{5,21},{6,22},{7,23},{8,24},{9,... | collective-permute-start | bytes 1572872 | tf_op jit(solution)/shard_map/ppermute | solution.py:902
  39.7 28.4 %collective-permute-start.9 = (bf16[108,16,128]{2,1,0:T(8,128)(2,1)S(1)}, bf16[108,16,128]{2,1,0:T(8,128)(2,1)S(1)}, u32[]{:S(2)}, u32[]{:S(2)}) collective-permute-start(bf16[108,16,128]{2,1,0:T(8,128)(2,1)S(1)} %pad_maximum_fusion.9), channel_id=1, source_target_pairs={{0,8},{1,9},{2,10},{3,11},{4,12},{5,13},{6,14},{7,15},{8,0},{9,1},... | collective-permute-start | bytes 1327112 | tf_op jit(solution)/shard_map/ppermute | solution.py:902
  75.2 45.2 %collective-permute-start.16 = (bf16[2048,128]{1,0:T(8,128)(2,1)S(1)}, bf16[2048,128]{1,0:T(8,128)(2,1)S(1)}, u32[]{:S(2)}, u32[]{:S(2)}) collective-permute-start(bf16[2048,128]{1,0:T(8,128)(2,1)S(1)} %pad_maximum_fusion.8), channel_id=1, source_target_pairs={{0,6},{1,7},{2,4},{3,5},{4,2},{5,3},{6,0},{7,1},{8,14},{9,15},{10,... | collective-permute-start | bytes 1572872 | tf_op jit(solution)/shard_map/ppermute | solution.py:902
  86.3 37.1 %collective-permute-start.13 = (bf16[324,16,128]{2,1,0:T(8,128)(2,1)S(1)}, bf16[324,16,128]{2,1,0:T(8,128)(2,1)S(1)}, u32[]{:S(2)}, u32[]{:S(2)}) collective-permute-start(bf16[324,16,128]{2,1,0:T(8,128)(2,1)S(1)} %pad_maximum_fusion.1), channel_id=1, source_target_pairs={{0,8},{1,9},{2,10},{3,11},{4,12},{5,13},{6,14},{7,15},{8,0},{9,1},... | collective-permute-start | bytes 3981320 | tf_op jit(solution)/shard_map/ppermute | solution.py:902
  86.5 36.9 %collective-permute-start.11 = (bf16[324,16,128]{2,1,0:T(8,128)(2,1)S(1)}, bf16[324,16,128]{2,1,0:T(8,128)(2,1)}, u32[]{:S(2)}, u32[]{:S(2)}) collective-permute-start(bf16[324,16,128]{2,1,0:T(8,128)(2,1)S(1)} %pad_maximum_fusion), channel_id=1, source_target_pairs={{0,16},{1,17},{2,18},{3,19},{4,20},{5,21},{6,22},{7,23},{8,24},{9,... | collective-permute-start | bytes 3981320 | tf_op jit(solution)/shard_map/ppermute | solution.py:902
  126.3 40.1 %collective-permute-start.17 = (bf16[216,16,128]{2,1,0:T(8,128)(2,1)S(1)}, bf16[216,16,128]{2,1,0:T(8,128)(2,1)}, u32[]{:S(2)}, u32[]{:S(2)}) collective-permute-start(bf16[216,16,128]{2,1,0:T(8,128)(2,1)S(1)} %pad_maximum_fusion.3), channel_id=1, source_target_pairs={{0,8},{1,9},{2,10},{3,11},{4,12},{5,13},{6,14},{7,15},{8,0},{9,1},... | collective-permute-start | bytes 2654216 | tf_op jit(solution)/shard_map/ppermute | solution.py:902
  126.4 40.0 %collective-permute-start.18 = (bf16[216,16,128]{2,1,0:T(8,128)(2,1)S(1)}, bf16[216,16,128]{2,1,0:T(8,128)(2,1)}, u32[]{:S(2)}, u32[]{:S(2)}) collective-permute-start(bf16[216,16,128]{2,1,0:T(8,128)(2,1)S(1)} %pad_maximum_fusion.4), channel_id=1, source_target_pairs={{0,16},{1,17},{2,18},{3,19},{4,20},{5,21},{6,22},{7,23},{8,24},{9,... | collective-permute-start | bytes 2654216 | tf_op jit(solution)/shard_map/ppermute | solution.py:902
  136.5 29.9 %collective-permute-start.22 = (bf16[216,16,128]{2,1,0:T(8,128)(2,1)S(1)}, bf16[216,16,128]{2,1,0:T(8,128)(2,1)}, u32[]{:S(2)}, u32[]{:S(2)}) collective-permute-start(bf16[216,16,128]{2,1,0:T(8,128)(2,1)S(1)} %pad_maximum_fusion.3), channel_id=1, source_target_pairs={{0,16},{1,17},{2,18},{3,19},{4,20},{5,21},{6,22},{7,23},{8,24},{9,... | collective-permute-start | bytes 2654216 | tf_op jit(solution)/shard_map/ppermute | solution.py:902
  136.5 30.1 %collective-permute-start.23 = (bf16[216,16,128]{2,1,0:T(8,128)(2,1)S(1)}, bf16[216,16,128]{2,1,0:T(8,128)(2,1)}, u32[]{:S(2)}, u32[]{:S(2)}) collective-permute-start(bf16[216,16,128]{2,1,0:T(8,128)(2,1)S(1)} %pad_maximum_fusion.4), channel_id=1, source_target_pairs={{0,8},{1,9},{2,10},{3,11},{4,12},{5,13},{6,14},{7,15},{8,0},{9,1},... | collective-permute-start | bytes 2654216 | tf_op jit(solution)/shard_map/ppermute | solution.py:902
  139.7 53.5 %collective-permute-start.30 = (bf16[432,16,128]{2,1,0:T(8,128)(2,1)S(1)}, bf16[432,16,128]{2,1,0:T(8,128)(2,1)S(1)}, u32[]{:S(2)}, u32[]{:S(2)}) collective-permute-start(bf16[432,16,128]{2,1,0:T(8,128)(2,1)S(1)} %constant_dynamic-update-slice_fusion.10.refs_8_), channel_id=1, source_target_pairs={{0,1},{1,0},{2,3},{3,2},{4,5},{5,4},{6,7},{7,6},{8,9},{9,8},{10,11... | collective-permute-start | bytes 5308424 | tf_op jit(solution)/shard_map/ppermute | solution.py:902
  286.5 40.1 %collective-permute-start.36 = (bf16[432,16,128]{2,1,0:T(8,128)(2,1)}, bf16[432,16,128]{2,1,0:T(8,128)(2,1)S(1)}, u32[]{:S(2)}, u32[]{:S(2)}) collective-permute-start(bf16[432,16,128]{2,1,0:T(8,128)(2,1)} %get-tuple-element.305), channel_id=1, source_target_pairs={{0,16},{1,17},{2,18},{3,19},{4,20},{5,21},{6,22},{7,23},{8,24},{9,... | collective-permute-start | bytes 5308424 | tf_op jit(solution)/shard_map/ppermute | solution.py:902
  287.1 39.7 %collective-permute-start.35 = (bf16[432,16,128]{2,1,0:T(8,128)(2,1)}, bf16[432,16,128]{2,1,0:T(8,128)(2,1)S(1)}, u32[]{:S(2)}, u32[]{:S(2)}) collective-permute-start(bf16[432,16,128]{2,1,0:T(8,128)(2,1)} %get-tuple-element.300), channel_id=1, source_target_pairs={{0,8},{1,9},{2,10},{3,11},{4,12},{5,13},{6,14},{7,15},{8,0},{9,1},... | collective-permute-start | bytes 5308424 | tf_op jit(solution)/shard_map/ppermute | solution.py:902
  341.6 47.3 %collective-permute-start.40 = (bf16[432,16,128]{2,1,0:T(8,128)(2,1)}, bf16[432,16,128]{2,1,0:T(8,128)(2,1)}, u32[]{:S(2)}, u32[]{:S(2)}) collective-permute-start(bf16[432,16,128]{2,1,0:T(8,128)(2,1)} %get-tuple-element.349), channel_id=1, source_target_pairs={{0,16},{1,17},{2,18},{3,19},{4,20},{5,21},{6,22},{7,23},{8,24},{9,... | collective-permute-start | bytes 5308424 | tf_op jit(solution)/shard_map/ppermute | solution.py:902
  342.5 46.4 %collective-permute-start.39 = (bf16[432,16,128]{2,1,0:T(8,128)(2,1)}, bf16[432,16,128]{2,1,0:T(8,128)(2,1)}, u32[]{:S(2)}, u32[]{:S(2)}) collective-permute-start(bf16[432,16,128]{2,1,0:T(8,128)(2,1)} %get-tuple-element.341), channel_id=1, source_target_pairs={{0,8},{1,9},{2,10},{3,11},{4,12},{5,13},{6,14},{7,15},{8,0},{9,1},... | collective-permute-start | bytes 5308424 | tf_op jit(solution)/shard_map/ppermute | solution.py:902
  353.5 31.9 %collective-permute-start.45 = (bf16[108,16,128]{2,1,0:T(8,128)(2,1)}, bf16[108,16,128]{2,1,0:T(8,128)(2,1)}, u32[]{:S(2)}, u32[]{:S(2)}) collective-permute-start(bf16[108,16,128]{2,1,0:T(8,128)(2,1)} %pad_maximum_fusion.13), channel_id=1, source_target_pairs={{0,6},{1,7},{2,4},{3,5},{4,2},{5,3},{6,0},{7,1},{8,14},{9,15},{10,... | collective-permute-start | bytes 1327112 | tf_op jit(solution)/shard_map/ppermute | solution.py:902
  355.4 29.9 %collective-permute-start.44 = (bf16[108,16,128]{2,1,0:T(8,128)(2,1)}, bf16[108,16,128]{2,1,0:T(8,128)(2,1)}, u32[]{:S(2)}, u32[]{:S(2)}) collective-permute-start(bf16[108,16,128]{2,1,0:T(8,128)(2,1)} %pad_maximum_fusion.12), channel_id=1, source_target_pairs={{0,4},{1,5},{2,6},{3,7},{4,0},{5,1},{6,2},{7,3},{8,12},{9,13},{10,... | collective-permute-start | bytes 1327112 | tf_op jit(solution)/shard_map/ppermute | solution.py:902
  356.3 29.1 %collective-permute-start.43 = (bf16[108,16,128]{2,1,0:T(8,128)(2,1)}, bf16[108,16,128]{2,1,0:T(8,128)(2,1)}, u32[]{:S(2)}, u32[]{:S(2)}) collective-permute-start(bf16[108,16,128]{2,1,0:T(8,128)(2,1)} %pad_maximum_fusion.11), channel_id=1, source_target_pairs={{0,2},{1,3},{2,0},{3,1},{4,6},{5,7},{6,4},{7,5},{8,10},{9,11},{10,... | collective-permute-start | bytes 1327112 | tf_op jit(solution)/shard_map/ppermute | solution.py:902
  414.1 46.0 %collective-permute-start.53 = (bf16[108,16,128]{2,1,0:T(8,128)(2,1)S(1)}, bf16[108,16,128]{2,1,0:T(8,128)(2,1)S(1)}, u32[]{:S(2)}, u32[]{:S(2)}) collective-permute-start(bf16[108,16,128]{2,1,0:T(8,128)(2,1)S(1)} %pad_maximum_fusion.17), channel_id=1, source_target_pairs={{0,6},{1,7},{2,4},{3,5},{4,2},{5,3},{6,0},{7,1},{8,14},{9,15},{10,... | collective-permute-start | bytes 1327112 | tf_op jit(solution)/shard_map/ppermute | solution.py:902
  415.4 44.8 %collective-permute-start.52 = (bf16[108,16,128]{2,1,0:T(8,128)(2,1)S(1)}, bf16[108,16,128]{2,1,0:T(8,128)(2,1)S(1)}, u32[]{:S(2)}, u32[]{:S(2)}) collective-permute-start(bf16[108,16,128]{2,1,0:T(8,128)(2,1)S(1)} %pad_maximum_fusion.16), channel_id=1, source_target_pairs={{0,4},{1,5},{2,6},{3,7},{4,0},{5,1},{6,2},{7,3},{8,12},{9,13},{10,... | collective-permute-start | bytes 1327112 | tf_op jit(solution)/shard_map/ppermute | solution.py:902
  417.7 42.5 %collective-permute-start.51 = (bf16[108,16,128]{2,1,0:T(8,128)(2,1)S(1)}, bf16[108,16,128]{2,1,0:T(8,128)(2,1)S(1)}, u32[]{:S(2)}, u32[]{:S(2)}) collective-permute-start(bf16[108,16,128]{2,1,0:T(8,128)(2,1)S(1)} %pad_maximum_fusion.15), channel_id=1, source_target_pairs={{0,2},{1,3},{2,0},{3,1},{4,6},{5,7},{6,4},{7,5},{8,10},{9,11},{10,... | collective-permute-start | bytes 1327112 | tf_op jit(solution)/shard_map/ppermute | solution.py:902
  422.6 33.8 %collective-permute-start.56 = (bf16[384,128]{1,0:T(8,128)(2,1)S(1)}, bf16[384,128]{1,0:T(8,128)(2,1)S(1)}, u32[]{:S(2)}, u32[]{:S(2)}) collective-permute-start(bf16[384,128]{1,0:T(8,128)(2,1)S(1)} %bitcast.124), channel_id=1, source_target_pairs={{0,1},{1,2},{2,3},{3,4},{4,5},{5,6},{6,7},{7,8},{8,9},{9,10},{10,1... | collective-permute-start | bytes 294920 | tf_op jit(solution)/shard_map/ppermute | solution.py:116
  430.6 25.7 %collective-permute-start.57 = (bf16[288,128]{1,0:T(8,128)(2,1)S(1)}, bf16[288,128]{1,0:T(8,128)(2,1)S(1)}, u32[]{:S(2)}, u32[]{:S(2)}) collective-permute-start(bf16[288,128]{1,0:T(8,128)(2,1)S(1)} %bitcast.126), channel_id=1, source_target_pairs={{1,0},{2,1},{3,2},{4,3},{5,4},{6,5},{7,6},{8,7},{9,8},{10,9},{11,1... | collective-permute-start | bytes 221192 | tf_op jit(solution)/shard_map/ppermute | solution.py:120
  (60 other events, 617.9 us)

commit v2 on v1

--- a/solution.py
+++ b/solution.py
@@ -876,9 +876,21 @@
     )(*ins, tiles)
 
 
+def pad_kernel(images_ref, rows_ref):
+    rows_ref[:SEQ] = images_ref[0].astype(jnp.float32)
+    rows_ref[SEQ:] = jnp.zeros((ROWS - SEQ, D), jnp.float32)
+
+
 def pad_rows(images):
-    padded = jnp.pad(images, ((0, 0), (0, ROWS - SEQ), (0, 0)))
-    return padded.reshape(-1, D).astype(jnp.float32)
+    count = images.shape[0]
+    return pl.pallas_call(
+        pad_kernel,
+        grid=(count,),
+        in_specs=[pl.BlockSpec((1, SEQ, D), lambda i: (i, 0, 0))],
+        out_specs=pl.BlockSpec((ROWS, D), lambda i: (i, 0)),
+        out_shape=jax.ShapeDtypeStruct((count * ROWS, D), jnp.float32),
+        name="pad_rows",
+    )(images)
 
 
 def cut_rows(rows):
@@ -1105,6 +1117,7 @@
     owned = Owned([params_first, params_second], me, devices)
     own = owned.share(0)
     small_rows = owned.small_rows(own)
+    tokens, cotangent, small_rows = tie(tokens, cotangent, small_rows)
     hidden, grad_output = pad_rows(tokens), pad_rows(cotangent)
 
     if stepwise:

time: 482 us -> 474 us (0.983)
  waiting for transfers between devices: 140 us -> 128 us
  Pallas kernels: 183 us -> 188 us
    ppermute x54, waiting for transfers between devices: 117 us -> 106 us  [exchange(): return lax.ppermute(block, AXES, perm)]
    unnamed x63 -> x65, local copies, waits for them, and re-layouts: 11.4 us -> 11.5 us
  transfers between devices with their start and end apart: 60 -> 60, of which waited for: 28 -> 27; matrix products, arithmetic and copies ran while one was open for 13% -> 13% of each run, Pallas kernels for 23% -> 25%
where the time goes in v2:
time: 474 us; the launch traced here: 467 us
  Pallas kernels  188 us (40%)
  waiting for transfers between devices  128 us (27%)
  starting transfers between devices  70.7 us (15%)
  other arithmetic  36.1 us (8%)
  local copies, waits for them, and re-layouts  29.4 us (6%)
  matrix products  13.4 us (3%)
    ppermute x54, waiting for transfers between devices, exchange(): return lax.ppermute(block, AXES, perm)  106 us
    ppermute x54, starting transfers between devices, exchange(): return lax.ppermute(block, AXES, perm)  49.2 us
    pallas_call x2, Pallas kernels, project(): pl.pallas_call(functools.partial(project_kernel, places, slots), grid_spe...  28.4 us
    pallas_call x2, Pallas kernels, mlp_back(): pl.pallas_call(mlp_back_kernel, grid=(1,), in_specs=[whole_spec(array.sha...  26.7 us
    pallas_call x2, Pallas kernels, mlp(): pl.pallas_call(mlp_kernel, grid=(1,), in_specs=[whole_spec(array.shape) f...  26.5 us
    pallas_call x2, Pallas kernels, weight_back(): pl.pallas_call(functools.partial(weight_back_kernel, places, stepwise), g...  25.7 us
    ppermute x3, waiting for transfers between devices, halo(): pieces.append(lax.ppermute(block[..., :take, :], AXES, perm))  21.8 us
    pallas_call x2, Pallas kernels, attention_back(): pl.pallas_call(functools.partial(attention_back_kernel, pairs), grid=(ste...  21.7 us
  transfers between devices with their start and end apart: 60, of which 27 were waited for; matrix products, arithmetic and copies ran while one was open for 13% of the time, Pallas kernels for 25%

profile of v2, /device:TPU:11, one launch (start us, length us, event | category | flops | bytes accessed | tf_op | source)
XLA Modules:
  0.0 467.4 jit_solution(13121232122856063081)
XLA Ops:
  40.3 10.7 %collective-permute-done.7 = bf16[108,16,128]{2,1,0:T(8,128)(2,1)S(1)} collective-permute-done((bf16[108,16,128]{2,1,0:T(8,128)(2,1)S(1)}, bf16[108,16,128]{2,1,0:T(8,128)(2,1)S(1)}, u32[]{:S(2)}, u32[]{:S(2)}) %collective-permute-start.7) | collective-permute-done | bytes 442400 | tf_op jit(solution)/shard_map/ppermute | solution.py:914
  51.1 9.4 %collective-permute-done.8 = bf16[108,16,128]{2,1,0:T(8,128)(2,1)S(1)} collective-permute-done((bf16[108,16,128]{2,1,0:T(8,128)(2,1)S(1)}, bf16[108,16,128]{2,1,0:T(8,128)(2,1)S(1)}, u32[]{:S(2)}, u32[]{:S(2)}) %collective-permute-start.8) | collective-permute-done | bytes 442400 | tf_op jit(solution)/shard_map/ppermute | solution.py:914
  70.6 9.6 %collective-permute-done.12 = bf16[162,16,128]{2,1,0:T(8,128)(2,1)S(1)} collective-permute-done((bf16[162,16,128]{2,1,0:T(8,128)(2,1)S(1)}, bf16[162,16,128]{2,1,0:T(8,128)(2,1)S(1)}, u32[]{:S(2)}, u32[]{:S(2)}) %collective-permute-start.12) | collective-permute-done | bytes 663584 | tf_op jit(solution)/shard_map/ppermute | solution.py:914
  91.1 22.4 %collective-permute-done.16 = bf16[2048,128]{1,0:T(8,128)(2,1)S(1)} collective-permute-done((bf16[2048,128]{1,0:T(8,128)(2,1)S(1)}, bf16[2048,128]{1,0:T(8,128)(2,1)S(1)}, u32[]{:S(2)}, u32[]{:S(2)}) %collective-permute-start.16) | collective-permute-done | bytes 524320 | tf_op jit(solution)/shard_map/ppermute | solution.py:914
  121.7 7.8 %collective-permute-done.20.refs_4_ = bf16[324,16,128]{2,1,0:T(8,128)(2,1)} collective-permute-done((bf16[324,16,128]{2,1,0:T(8,128)(2,1)}, bf16[324,16,128]{2,1,0:T(8,128)(2,1)}, u32[]{:S(2)}, u32[]{:S(2)}) %collective-permute-start.20) | collective-permute-done | bytes 1327136 | tf_op jit(solution)/shard_map/ppermute | solution.py:914
  136.0 14.2 %project.2 = (bf16[416,768]{1,0:T(8,128)(2,1)}, bf16[416,2304]{1,0:T(8,128)(2,1)}, bf16[3456,16,128]{2,1,0:T(8,128)(2,1)}) custom-call(s32[4]{0:T(128)} %pad_add_fusion.at_ref, bf16[1080,16,128]{2,1,0:T(8,128)(2,1)} %constant_dynamic-update-slice_fusion.refs_0_, bf16[1080,16,128]{2,1,0:T(8,128)(2,1)} %collective-permute-done.19.refs_1_, ...), custom_call_target="tpu_custom_call" | custom-call | tf_op jit(solution)/shard_map/project/pallas_call | solution.py:562
  156.3 5.8 %bias.3.bias_ref = f32[12,208,208]{2,1,0:T(8,128)} custom-call(bf16[16,768]{1,0:T(8,128)(2,1)} %get-tuple-element.456.entries_ref), custom_call_target="tpu_custom_call" | custom-call | tf_op jit(solution)/shard_map/bias/pallas_call | solution.py:268
  166.2 7.4 %attention.2 = (bf16[416,768]{1,0:T(8,128)(2,1)}, bf16[2,12,208,208]{3,2,1,0:T(8,128)(2,1)}) custom-call(s32[2]{0:T(128)} %counts_ref.3, bf16[416,2304]{1,0:T(8,128)(2,1)} %get-tuple-element.250.query_ref.key_ref.value_ref, bf16[416,2304]{1,0:T(8,128)(2,1)} %get-tuple-element.250.query_ref.key_ref.value_ref, ...), custom_call_target="tpu_custom_call" | custom-call | tf_op jit(solution)/shard_map/attention/pallas_call | solution.py:413
  173.6 13.3 %mlp.2 = (f32[416,768]{1,0:T(8,128)}, bf16[416,768]{1,0:T(8,128)(2,1)}, f32[416,768]{1,0:T(8,128)}, bf16[416,768]{1,0:T(8,128)(2,1)}, bf16[416,3072]{1,0:T(8,128...) custom-call(bf16[416,768]{1,0:T(8,128)(2,1)} %get-tuple-element.252.attended_ref.refs_2_, ...), custom_call_target="tpu_custom_call" | custom-call | tf_op jit(solution)/shard_map/mlp/pallas_call | solution.py:672
  193.0 14.2 %project.3 = (bf16[416,768]{1,0:T(8,128)(2,1)}, bf16[416,2304]{1,0:T(8,128)(2,1)}, bf16[3456,16,128]{2,1,0:T(8,128)(2,1)}) custom-call(s32[4]{0:T(128)} %pad_add_fusion.at_ref, bf16[216,16,128]{2,1,0:T(8,128)(2,1)} %collective-permute-done.17.refs_0_, bf16[216,16,128]{2,1,0:T(8,128)(2,1)} %collective-permute-done.18.refs_1_, ...), custom_call_target="tpu_custom_call" | custom-call | tf_op jit(solution)/shard_map/project/pallas_call | solution.py:562
  207.2 7.6 %attention.3 = (bf16[416,768]{1,0:T(8,128)(2,1)}, bf16[2,12,208,208]{3,2,1,0:T(8,128)(2,1)}) custom-call(s32[2]{0:T(128)} %counts_ref.3, bf16[416,2304]{1,0:T(8,128)(2,1)} %get-tuple-element.279.query_ref.key_ref.value_ref, bf16[416,2304]{1,0:T(8,128)(2,1)} %get-tuple-element.279.query_ref.key_ref.value_ref, ...), custom_call_target="tpu_custom_call" | custom-call | tf_op jit(solution)/shard_map/attention/pallas_call | solution.py:413
  214.8 13.2 %mlp.3 = (f32[416,768]{1,0:T(8,128)}, bf16[416,768]{1,0:T(8,128)(2,1)}, f32[416,768]{1,0:T(8,128)}, bf16[416,768]{1,0:T(8,128)(2,1)}, bf16[416,3072]{1,0:T(8,128...) custom-call(bf16[416,768]{1,0:T(8,128)(2,1)} %get-tuple-element.282.attended_ref.refs_2_, ...), custom_call_target="tpu_custom_call" | custom-call | tf_op jit(solution)/shard_map/mlp/pallas_call | solution.py:672
  228.0 13.6 %mlp_back.2 = (f32[416,768]{1,0:T(8,128)}, bf16[416,768]{1,0:T(8,128)(2,1)}, bf16[416,768]{1,0:T(8,128)(2,1)}, bf16[416,3072]{1,0:T(8,128)(2,1)}, bf16[416,768]{1,0:T(8,128)(2,1)}, /*index=5*/f32[64,128]{1,0:T(8,128)}) custom-call(f32[416,768]{1,0:T(8,128)} %pad_rows.3.grad_ref, bf16[416,768]{1,0:T(8,128)(2,1)} %get-tuple-element.284.branch_ref, ...), custom_call_target="tpu_custom_call" | custom-call | tf_op jit(solution)/shard_map/mlp_back/pallas_call | solution.py:744
  241.5 10.9 %attention_back.2 = (bf16[3,416,768]{2,1,0:T(8,128)(2,1)}, f32[12,208,208]{2,1,0:T(8,128)}) custom-call(bf16[416,2304]{1,0:T(8,128)(2,1)} %get-tuple-element.279.query_ref.key_ref.value_ref, bf16[416,2304]{1,0:T(8,128)(2,1)} %get-tuple-element.279.query_ref.key_ref.value_ref, bf16[416,2304]{1,0:T(8,128)(2,1)} %get-tuple-element.279.query_ref.key_ref.value_ref, ...), custom_call_target="tpu_custom_call" | custom-call | tf_op jit(solution)/shard_map/attention_back/pallas_call | solution.py:433
  252.4 12.8 %weight_back.2 = (bf16[864,16,128]{2,1,0:T(8,128)(2,1)}, bf16[864,16,128]{2,1,0:T(8,128)(2,1)}, bf16[864,16,128]{2,1,0:T(8,128)(2,1)}, bf16[864,16,128]{2,1,0:T(8,128)(2,1)}) custom-call(s32[4]{0:T(128)} %pad_add_fusion.at_ref, bf16[416,768]{1,0:T(8,128)(2,1)} %get-tuple-element.278.refs_0_, bf16[3,416,768]{2,1,0:T(8,128)(2,1)} %get-tuple-element.290.refs_1_.project_ref, ...), custom_call_target="tpu_custom_call" | custom-call | tf_op jit(solution)/shard_map/weight_back/pallas_call | solution.py:827
  265.8 6.7 %input_back.2 = (f32[416,768]{1,0:T(8,128)}, f32[24,128]{1,0:T(8,128)}) custom-call(bf16[3,416,768]{2,1,0:T(8,128)(2,1)} %get-tuple-element.290.refs_1_.project_ref, f32[416,768]{1,0:T(8,128)} %get-tuple-element.300.grad_middle_ref, f32[416,768]{1,0:T(8,128)} %get-tuple-element.277.refs_14_.hidden_ref, f32[160,128]{1,0:T(8,128)} %get-tuple-element.452.refs_15_.vectors_ref, ...), custom_call_target="tpu_custom_call" | custom-call | tf_op jit(solution)/shard_map/input_back/pallas_call | solution.py:867
  281.9 13.1 %mlp_back.3 = (f32[416,768]{1,0:T(8,128)}, bf16[416,768]{1,0:T(8,128)(2,1)}, bf16[416,768]{1,0:T(8,128)(2,1)}, bf16[416,3072]{1,0:T(8,128)(2,1)}, bf16[416,768]{1,0:T(8,128)(2,1)}, /*index=5*/f32[64,128]{1,0:T(8,128)}) custom-call(f32[416,768]{1,0:T(8,128)} %get-tuple-element.313.grad_ref, bf16[416,768]{1,0:T(8,128)(2,1)} %get-tuple-element.314.branch_ref, ...), custom_call_target="tpu_custom_call" | custom-call | tf_op jit(solution)/shard_map/mlp_back/pallas_call | solution.py:744
  295.1 10.9 %attention_back.3 = (bf16[3,416,768]{2,1,0:T(8,128)(2,1)}, f32[12,208,208]{2,1,0:T(8,128)}) custom-call(bf16[416,2304]{1,0:T(8,128)(2,1)} %get-tuple-element.250.query_ref.key_ref.value_ref, bf16[416,2304]{1,0:T(8,128)(2,1)} %get-tuple-element.250.query_ref.key_ref.value_ref, bf16[416,2304]{1,0:T(8,128)(2,1)} %get-tuple-element.250.query_ref.key_ref.value_ref, ...), custom_call_target="tpu_custom_call" | custom-call | tf_op jit(solution)/shard_map/attention_back/pallas_call | solution.py:433
  305.9 12.9 %weight_back.3 = (bf16[864,16,128]{2,1,0:T(8,128)(2,1)}, bf16[864,16,128]{2,1,0:T(8,128)(2,1)}, bf16[864,16,128]{2,1,0:T(8,128)(2,1)}, bf16[864,16,128]{2,1,0:T(8,128)(2,1)}) custom-call(s32[4]{0:T(128)} %pad_add_fusion.at_ref, bf16[416,768]{1,0:T(8,128)(2,1)} %get-tuple-element.312.refs_0_, bf16[3,416,768]{2,1,0:T(8,128)(2,1)} %get-tuple-element.368.refs_1_.project_ref, ...), custom_call_target="tpu_custom_call" | custom-call | tf_op jit(solution)/shard_map/weight_back/pallas_call | solution.py:827
  337.4 6.5 %collective-permute-done.42 = bf16[216,16,128]{2,1,0:T(8,128)(2,1)S(1)} collective-permute-done((bf16[216,16,128]{2,1,0:T(8,128)(2,1)S(1)}, bf16[216,16,128]{2,1,0:T(8,128)(2,1)S(1)}, u32[]{:S(2)}, u32[]{:S(2)}) %collective-permute-start.42) | collective-permute-done | bytes 884768 | tf_op jit(solution)/shard_map/ppermute | solution.py:914
  351.5 15.2 %table_back.1 = f32[32,768]{1,0:T(8,128)} custom-call(f32[12,208,208]{2,1,0:T(8,128)} %get-tuple-element.374.first_ref, f32[12,208,208]{2,1,0:T(8,128)} %get-tuple-element.375.second_ref), custom_call_target="tpu_custom_call" | custom-call | tf_op jit(solution)/shard_map/table_back/pallas_call | solution.py:319
  371.9 6.6 %input_back.3 = (f32[416,768]{1,0:T(8,128)}, f32[24,128]{1,0:T(8,128)}) custom-call(bf16[3,416,768]{2,1,0:T(8,128)(2,1)} %get-tuple-element.368.refs_1_.project_ref, f32[416,768]{1,0:T(8,128)} %get-tuple-element.369.grad_middle_ref, f32[416,768]{1,0:T(8,128)} %pad_rows.2.refs_6_.hidden_ref, f32[160,128]{1,0:T(8,128)} %get-tuple-element.453.refs_7_.vectors_ref, ...), custom_call_target="tpu_custom_call" | custom-call | tf_op jit(solution)/shard_map/input_back/pallas_call | solution.py:867
  416.8 8.2 %collective-permute-start.56 = (bf16[384,128]{1,0:T(8,128)(2,1)S(1)}, bf16[384,128]{1,0:T(8,128)(2,1)S(1)}, u32[]{:S(2)}, u32[]{:S(2)}) collective-permute-start(bf16[384,128]{1,0:T(8,128)(2,1)S(1)} %bitcast.118), channel_id=1, source_target_pairs={{0,1},{1,2},{2,3},{3,4},{4,5},{5,6},{6,7},{7,8},{8,9},{9,10},{10,1... | collective-permute-start | bytes 294920 | tf_op jit(solution)/shard_map/ppermute | solution.py:116
  429.6 20.5 %collective-permute-done.57 = bf16[288,128]{1,0:T(8,128)(2,1)S(1)} collective-permute-done((bf16[288,128]{1,0:T(8,128)(2,1)S(1)}, bf16[288,128]{1,0:T(8,128)(2,1)S(1)}, u32[]{:S(2)}, u32[]{:S(2)}) %collective-permute-start.57) | collective-permute-done | bytes 73760 | tf_op jit(solution)/shard_map/ppermute | solution.py:120
  (284 shorter events, 192.2 us)
Async XLA Ops:
  18.6 32.5 %collective-permute-start.7 = (bf16[108,16,128]{2,1,0:T(8,128)(2,1)S(1)}, bf16[108,16,128]{2,1,0:T(8,128)(2,1)S(1)}, u32[]{:S(2)}, u32[]{:S(2)}) collective-permute-start(bf16[108,16,128]{2,1,0:T(8,128)(2,1)S(1)} %bitcast.112), channel_id=1, source_target_pairs={{0,4},{1,5},{2,6},{3,7},{4,0},{5,1},{6,2},{7,3},{8,12},{9,13},{10,... | collective-permute-start | bytes 1327112 | tf_op jit(solution)/shard_map/ppermute | solution.py:914
  23.4 37.1 %collective-permute-start.8 = (bf16[108,16,128]{2,1,0:T(8,128)(2,1)S(1)}, bf16[108,16,128]{2,1,0:T(8,128)(2,1)S(1)}, u32[]{:S(2)}, u32[]{:S(2)}) collective-permute-start(bf16[108,16,128]{2,1,0:T(8,128)(2,1)S(1)} %bitcast.113), channel_id=1, source_target_pairs={{0,6},{1,7},{2,4},{3,5},{4,2},{5,3},{6,0},{7,1},{8,14},{9,15},{10,... | collective-permute-start | bytes 1327112 | tf_op jit(solution)/shard_map/ppermute | solution.py:914
  35.3 25.4 %collective-permute-start.4 = (bf16[128,16,128]{2,1,0:T(8,128)(2,1)S(1)}, bf16[128,16,128]{2,1,0:T(8,128)(2,1)S(1)}, u32[]{:S(2)}, u32[]{:S(2)}) collective-permute-start(bf16[128,16,128]{2,1,0:T(8,128)(2,1)S(1)} %pad_maximum_fusion.7), channel_id=1, source_target_pairs={{0,16},{1,17},{2,18},{3,19},{4,20},{5,21},{6,22},{7,23},{8,24},{9,... | collective-permute-start | bytes 1572872 | tf_op jit(solution)/shard_map/ppermute | solution.py:914
  36.3 27.2 %collective-permute-start.9 = (bf16[108,16,128]{2,1,0:T(8,128)(2,1)S(1)}, bf16[108,16,128]{2,1,0:T(8,128)(2,1)S(1)}, u32[]{:S(2)}, u32[]{:S(2)}) collective-permute-start(bf16[108,16,128]{2,1,0:T(8,128)(2,1)S(1)} %pad_maximum_fusion.9), channel_id=1, source_target_pairs={{0,8},{1,9},{2,10},{3,11},{4,12},{5,13},{6,14},{7,15},{8,0},{9,1},... | collective-permute-start | bytes 1327112 | tf_op jit(solution)/shard_map/ppermute | solution.py:914
  66.0 25.2 %collective-permute-start.15 = (bf16[2048,128]{1,0:T(8,128)(2,1)S(1)}, bf16[2048,128]{1,0:T(8,128)(2,1)S(1)}, u32[]{:S(2)}, u32[]{:S(2)}) collective-permute-start(bf16[2048,128]{1,0:T(8,128)(2,1)S(1)} %pad_maximum_fusion.8), channel_id=1, source_target_pairs={{0,4},{1,5},{2,6},{3,7},{4,0},{5,1},{6,2},{7,3},{8,12},{9,13},{10,... | collective-permute-start | bytes 1572872 | tf_op jit(solution)/shard_map/ppermute | solution.py:914
  68.4 45.1 %collective-permute-start.16 = (bf16[2048,128]{1,0:T(8,128)(2,1)S(1)}, bf16[2048,128]{1,0:T(8,128)(2,1)S(1)}, u32[]{:S(2)}, u32[]{:S(2)}) collective-permute-start(bf16[2048,128]{1,0:T(8,128)(2,1)S(1)} %pad_maximum_fusion.8), channel_id=1, source_target_pairs={{0,6},{1,7},{2,4},{3,5},{4,2},{5,3},{6,0},{7,1},{8,14},{9,15},{10,... | collective-permute-start | bytes 1572872 | tf_op jit(solution)/shard_map/ppermute | solution.py:914
  80.3 36.2 %collective-permute-start.13 = (bf16[324,16,128]{2,1,0:T(8,128)(2,1)S(1)}, bf16[324,16,128]{2,1,0:T(8,128)(2,1)S(1)}, u32[]{:S(2)}, u32[]{:S(2)}) collective-permute-start(bf16[324,16,128]{2,1,0:T(8,128)(2,1)S(1)} %pad_maximum_fusion.1), channel_id=1, source_target_pairs={{0,8},{1,9},{2,10},{3,11},{4,12},{5,13},{6,14},{7,15},{8,0},{9,1},... | collective-permute-start | bytes 3981320 | tf_op jit(solution)/shard_map/ppermute | solution.py:914
  81.6 34.9 %collective-permute-start.11 = (bf16[324,16,128]{2,1,0:T(8,128)(2,1)S(1)}, bf16[324,16,128]{2,1,0:T(8,128)(2,1)}, u32[]{:S(2)}, u32[]{:S(2)}) collective-permute-start(bf16[324,16,128]{2,1,0:T(8,128)(2,1)S(1)} %pad_maximum_fusion), channel_id=1, source_target_pairs={{0,16},{1,17},{2,18},{3,19},{4,20},{5,21},{6,22},{7,23},{8,24},{9,... | collective-permute-start | bytes 3981320 | tf_op jit(solution)/shard_map/ppermute | solution.py:914
  119.4 42.7 %collective-permute-start.17 = (bf16[216,16,128]{2,1,0:T(8,128)(2,1)S(1)}, bf16[216,16,128]{2,1,0:T(8,128)(2,1)}, u32[]{:S(2)}, u32[]{:S(2)}) collective-permute-start(bf16[216,16,128]{2,1,0:T(8,128)(2,1)S(1)} %pad_maximum_fusion.3), channel_id=1, source_target_pairs={{0,8},{1,9},{2,10},{3,11},{4,12},{5,13},{6,14},{7,15},{8,0},{9,1},... | collective-permute-start | bytes 2654216 | tf_op jit(solution)/shard_map/ppermute | solution.py:914
  120.3 41.8 %collective-permute-start.18 = (bf16[216,16,128]{2,1,0:T(8,128)(2,1)S(1)}, bf16[216,16,128]{2,1,0:T(8,128)(2,1)}, u32[]{:S(2)}, u32[]{:S(2)}) collective-permute-start(bf16[216,16,128]{2,1,0:T(8,128)(2,1)S(1)} %pad_maximum_fusion.4), channel_id=1, source_target_pairs={{0,16},{1,17},{2,18},{3,19},{4,20},{5,21},{6,22},{7,23},{8,24},{9,... | collective-permute-start | bytes 2654216 | tf_op jit(solution)/shard_map/ppermute | solution.py:914
  129.5 32.6 %collective-permute-start.22 = (bf16[216,16,128]{2,1,0:T(8,128)(2,1)S(1)}, bf16[216,16,128]{2,1,0:T(8,128)(2,1)}, u32[]{:S(2)}, u32[]{:S(2)}) collective-permute-start(bf16[216,16,128]{2,1,0:T(8,128)(2,1)S(1)} %pad_maximum_fusion.3), channel_id=1, source_target_pairs={{0,16},{1,17},{2,18},{3,19},{4,20},{5,21},{6,22},{7,23},{8,24},{9,... | collective-permute-start | bytes 2654216 | tf_op jit(solution)/shard_map/ppermute | solution.py:914
  130.5 31.6 %collective-permute-start.23 = (bf16[216,16,128]{2,1,0:T(8,128)(2,1)S(1)}, bf16[216,16,128]{2,1,0:T(8,128)(2,1)}, u32[]{:S(2)}, u32[]{:S(2)}) collective-permute-start(bf16[216,16,128]{2,1,0:T(8,128)(2,1)S(1)} %pad_maximum_fusion.4), channel_id=1, source_target_pairs={{0,8},{1,9},{2,10},{3,11},{4,12},{5,13},{6,14},{7,15},{8,0},{9,1},... | collective-permute-start | bytes 2654216 | tf_op jit(solution)/shard_map/ppermute | solution.py:914
  135.0 52.0 %collective-permute-start.30 = (bf16[432,16,128]{2,1,0:T(8,128)(2,1)S(1)}, bf16[432,16,128]{2,1,0:T(8,128)(2,1)S(1)}, u32[]{:S(2)}, u32[]{:S(2)}) collective-permute-start(bf16[432,16,128]{2,1,0:T(8,128)(2,1)S(1)} %constant_dynamic-update-slice_fusion.10.refs_8_), channel_id=1, source_target_pairs={{0,1},{1,0},{2,3},{3,2},{4,5},{5,4},{6,7},{7,6},{8,9},{9,8},{10,11... | collective-permute-start | bytes 5308424 | tf_op jit(solution)/shard_map/ppermute | solution.py:914
  281.1 40.0 %collective-permute-start.36 = (bf16[432,16,128]{2,1,0:T(8,128)(2,1)}, bf16[432,16,128]{2,1,0:T(8,128)(2,1)S(1)}, u32[]{:S(2)}, u32[]{:S(2)}) collective-permute-start(bf16[432,16,128]{2,1,0:T(8,128)(2,1)} %get-tuple-element.311), channel_id=1, source_target_pairs={{0,16},{1,17},{2,18},{3,19},{4,20},{5,21},{6,22},{7,23},{8,24},{9,... | collective-permute-start | bytes 5308424 | tf_op jit(solution)/shard_map/ppermute | solution.py:914
  281.4 39.7 %collective-permute-start.35 = (bf16[432,16,128]{2,1,0:T(8,128)(2,1)}, bf16[432,16,128]{2,1,0:T(8,128)(2,1)S(1)}, u32[]{:S(2)}, u32[]{:S(2)}) collective-permute-start(bf16[432,16,128]{2,1,0:T(8,128)(2,1)} %get-tuple-element.306), channel_id=1, source_target_pairs={{0,8},{1,9},{2,10},{3,11},{4,12},{5,13},{6,14},{7,15},{8,0},{9,1},... | collective-permute-start | bytes 5308424 | tf_op jit(solution)/shard_map/ppermute | solution.py:914
  335.9 46.8 %collective-permute-start.40 = (bf16[432,16,128]{2,1,0:T(8,128)(2,1)}, bf16[432,16,128]{2,1,0:T(8,128)(2,1)}, u32[]{:S(2)}, u32[]{:S(2)}) collective-permute-start(bf16[432,16,128]{2,1,0:T(8,128)(2,1)} %get-tuple-element.355), channel_id=1, source_target_pairs={{0,16},{1,17},{2,18},{3,19},{4,20},{5,21},{6,22},{7,23},{8,24},{9,... | collective-permute-start | bytes 5308424 | tf_op jit(solution)/shard_map/ppermute | solution.py:914
  337.0 45.7 %collective-permute-start.39 = (bf16[432,16,128]{2,1,0:T(8,128)(2,1)}, bf16[432,16,128]{2,1,0:T(8,128)(2,1)}, u32[]{:S(2)}, u32[]{:S(2)}) collective-permute-start(bf16[432,16,128]{2,1,0:T(8,128)(2,1)} %get-tuple-element.347), channel_id=1, source_target_pairs={{0,8},{1,9},{2,10},{3,11},{4,12},{5,13},{6,14},{7,15},{8,0},{9,1},... | collective-permute-start | bytes 5308424 | tf_op jit(solution)/shard_map/ppermute | solution.py:914
  347.3 32.1 %collective-permute-start.45 = (bf16[108,16,128]{2,1,0:T(8,128)(2,1)}, bf16[108,16,128]{2,1,0:T(8,128)(2,1)}, u32[]{:S(2)}, u32[]{:S(2)}) collective-permute-start(bf16[108,16,128]{2,1,0:T(8,128)(2,1)} %pad_maximum_fusion.13), channel_id=1, source_target_pairs={{0,6},{1,7},{2,4},{3,5},{4,2},{5,3},{6,0},{7,1},{8,14},{9,15},{10,... | collective-permute-start | bytes 1327112 | tf_op jit(solution)/shard_map/ppermute | solution.py:914
  349.3 30.1 %collective-permute-start.44 = (bf16[108,16,128]{2,1,0:T(8,128)(2,1)}, bf16[108,16,128]{2,1,0:T(8,128)(2,1)}, u32[]{:S(2)}, u32[]{:S(2)}) collective-permute-start(bf16[108,16,128]{2,1,0:T(8,128)(2,1)} %pad_maximum_fusion.12), channel_id=1, source_target_pairs={{0,4},{1,5},{2,6},{3,7},{4,0},{5,1},{6,2},{7,3},{8,12},{9,13},{10,... | collective-permute-start | bytes 1327112 | tf_op jit(solution)/shard_map/ppermute | solution.py:914
  350.1 29.3 %collective-permute-start.43 = (bf16[108,16,128]{2,1,0:T(8,128)(2,1)}, bf16[108,16,128]{2,1,0:T(8,128)(2,1)}, u32[]{:S(2)}, u32[]{:S(2)}) collective-permute-start(bf16[108,16,128]{2,1,0:T(8,128)(2,1)} %pad_maximum_fusion.11), channel_id=1, source_target_pairs={{0,2},{1,3},{2,0},{3,1},{4,6},{5,7},{6,4},{7,5},{8,10},{9,11},{10,... | collective-permute-start | bytes 1327112 | tf_op jit(solution)/shard_map/ppermute | solution.py:914
  407.9 46.0 %collective-permute-start.53 = (bf16[108,16,128]{2,1,0:T(8,128)(2,1)S(1)}, bf16[108,16,128]{2,1,0:T(8,128)(2,1)S(1)}, u32[]{:S(2)}, u32[]{:S(2)}) collective-permute-start(bf16[108,16,128]{2,1,0:T(8,128)(2,1)S(1)} %pad_maximum_fusion.17), channel_id=1, source_target_pairs={{0,6},{1,7},{2,4},{3,5},{4,2},{5,3},{6,0},{7,1},{8,14},{9,15},{10,... | collective-permute-start | bytes 1327112 | tf_op jit(solution)/shard_map/ppermute | solution.py:914
  409.2 44.7 %collective-permute-start.52 = (bf16[108,16,128]{2,1,0:T(8,128)(2,1)S(1)}, bf16[108,16,128]{2,1,0:T(8,128)(2,1)S(1)}, u32[]{:S(2)}, u32[]{:S(2)}) collective-permute-start(bf16[108,16,128]{2,1,0:T(8,128)(2,1)S(1)} %pad_maximum_fusion.16), channel_id=1, source_target_pairs={{0,4},{1,5},{2,6},{3,7},{4,0},{5,1},{6,2},{7,3},{8,12},{9,13},{10,... | collective-permute-start | bytes 1327112 | tf_op jit(solution)/shard_map/ppermute | solution.py:914
  412.2 41.7 %collective-permute-start.51 = (bf16[108,16,128]{2,1,0:T(8,128)(2,1)S(1)}, bf16[108,16,128]{2,1,0:T(8,128)(2,1)S(1)}, u32[]{:S(2)}, u32[]{:S(2)}) collective-permute-start(bf16[108,16,128]{2,1,0:T(8,128)(2,1)S(1)} %pad_maximum_fusion.15), channel_id=1, source_target_pairs={{0,2},{1,3},{2,0},{3,1},{4,6},{5,7},{6,4},{7,5},{8,10},{9,11},{10,... | collective-permute-start | bytes 1327112 | tf_op jit(solution)/shard_map/ppermute | solution.py:914
  416.8 33.3 %collective-permute-start.56 = (bf16[384,128]{1,0:T(8,128)(2,1)S(1)}, bf16[384,128]{1,0:T(8,128)(2,1)S(1)}, u32[]{:S(2)}, u32[]{:S(2)}) collective-permute-start(bf16[384,128]{1,0:T(8,128)(2,1)S(1)} %bitcast.118), channel_id=1, source_target_pairs={{0,1},{1,2},{2,3},{3,4},{4,5},{5,6},{6,7},{7,8},{8,9},{9,10},{10,1... | collective-permute-start | bytes 294920 | tf_op jit(solution)/shard_map/ppermute | solution.py:116
  (61 other events, 617.3 us)

commit v3 on v2

--- a/solution.py
+++ b/solution.py
@@ -457,7 +457,7 @@
 
 FIRST = tile_starts()
 MLP_FIRST = FIRST["proj_weight"]
-SPAN = 1024
+SPAN = 1536
 
 
 def load_weight(ref, base, name, row, rows, column, columns):

time: 474 us -> 474 us (level)
  no operation moved by 1% of the time
where the time goes in v3:
time: 474 us; the launch traced here: 467 us
  Pallas kernels  187 us (39%)
  waiting for transfers between devices  129 us (27%)
  starting transfers between devices  70.4 us (15%)
  other arithmetic  36.1 us (8%)
  local copies, waits for them, and re-layouts  29.4 us (6%)
  matrix products  13.4 us (3%)
    ppermute x54, waiting for transfers between devices, exchange(): return lax.ppermute(block, AXES, perm)  106 us
    ppermute x54, starting transfers between devices, exchange(): return lax.ppermute(block, AXES, perm)  48.9 us
    pallas_call x2, Pallas kernels, project(): pl.pallas_call(functools.partial(project_kernel, places, slots), grid_spe...  28.4 us
    pallas_call x2, Pallas kernels, mlp(): pl.pallas_call(mlp_kernel, grid=(1,), in_specs=[whole_spec(array.shape) f...  26.4 us
    pallas_call x2, Pallas kernels, mlp_back(): pl.pallas_call(mlp_back_kernel, grid=(1,), in_specs=[whole_spec(array.sha...  26 us
    pallas_call x2, Pallas kernels, weight_back(): pl.pallas_call(functools.partial(weight_back_kernel, places, stepwise), g...  25.7 us
    ppermute x3, waiting for transfers between devices, halo(): pieces.append(lax.ppermute(block[..., :take, :], AXES, perm))  21.8 us
    pallas_call x2, Pallas kernels, attention_back(): pl.pallas_call(functools.partial(attention_back_kernel, pairs), grid=(ste...  21.7 us
  transfers between devices with their start and end apart: 60, of which 27 were waited for; matrix products, arithmetic and copies ran while one was open for 13% of the time, Pallas kernels for 25%

profile of v3, /device:TPU:11, one launch (start us, length us, event | category | flops | bytes accessed | tf_op | source)
XLA Modules:
  0.0 466.9 jit_solution(5671542640307705140)
XLA Ops:
  40.3 10.7 %collective-permute-done.7 = bf16[108,16,128]{2,1,0:T(8,128)(2,1)S(1)} collective-permute-done((bf16[108,16,128]{2,1,0:T(8,128)(2,1)S(1)}, bf16[108,16,128]{2,1,0:T(8,128)(2,1)S(1)}, u32[]{:S(2)}, u32[]{:S(2)}) %collective-permute-start.7) | collective-permute-done | bytes 442400 | tf_op jit(solution)/shard_map/ppermute | solution.py:914
  51.1 9.4 %collective-permute-done.8 = bf16[108,16,128]{2,1,0:T(8,128)(2,1)S(1)} collective-permute-done((bf16[108,16,128]{2,1,0:T(8,128)(2,1)S(1)}, bf16[108,16,128]{2,1,0:T(8,128)(2,1)S(1)}, u32[]{:S(2)}, u32[]{:S(2)}) %collective-permute-start.8) | collective-permute-done | bytes 442400 | tf_op jit(solution)/shard_map/ppermute | solution.py:914
  70.6 9.6 %collective-permute-done.12 = bf16[162,16,128]{2,1,0:T(8,128)(2,1)S(1)} collective-permute-done((bf16[162,16,128]{2,1,0:T(8,128)(2,1)S(1)}, bf16[162,16,128]{2,1,0:T(8,128)(2,1)S(1)}, u32[]{:S(2)}, u32[]{:S(2)}) %collective-permute-start.12) | collective-permute-done | bytes 663584 | tf_op jit(solution)/shard_map/ppermute | solution.py:914
  91.1 22.4 %collective-permute-done.16 = bf16[2048,128]{1,0:T(8,128)(2,1)S(1)} collective-permute-done((bf16[2048,128]{1,0:T(8,128)(2,1)S(1)}, bf16[2048,128]{1,0:T(8,128)(2,1)S(1)}, u32[]{:S(2)}, u32[]{:S(2)}) %collective-permute-start.16) | collective-permute-done | bytes 524320 | tf_op jit(solution)/shard_map/ppermute | solution.py:914
  121.7 7.8 %collective-permute-done.20.refs_4_ = bf16[324,16,128]{2,1,0:T(8,128)(2,1)} collective-permute-done((bf16[324,16,128]{2,1,0:T(8,128)(2,1)}, bf16[324,16,128]{2,1,0:T(8,128)(2,1)}, u32[]{:S(2)}, u32[]{:S(2)}) %collective-permute-start.20) | collective-permute-done | bytes 1327136 | tf_op jit(solution)/shard_map/ppermute | solution.py:914
  136.0 14.2 %project.2 = (bf16[416,768]{1,0:T(8,128)(2,1)}, bf16[416,2304]{1,0:T(8,128)(2,1)}, bf16[3456,16,128]{2,1,0:T(8,128)(2,1)}) custom-call(s32[4]{0:T(128)} %pad_add_fusion.at_ref, bf16[1080,16,128]{2,1,0:T(8,128)(2,1)} %constant_dynamic-update-slice_fusion.refs_0_, bf16[1080,16,128]{2,1,0:T(8,128)(2,1)} %collective-permute-done.19.refs_1_, ...), custom_call_target="tpu_custom_call" | custom-call | tf_op jit(solution)/shard_map/project/pallas_call | solution.py:562
  156.3 5.8 %bias.3.bias_ref = f32[12,208,208]{2,1,0:T(8,128)} custom-call(bf16[16,768]{1,0:T(8,128)(2,1)} %get-tuple-element.456.entries_ref), custom_call_target="tpu_custom_call" | custom-call | tf_op jit(solution)/shard_map/bias/pallas_call | solution.py:268
  166.2 7.4 %attention.2 = (bf16[416,768]{1,0:T(8,128)(2,1)}, bf16[2,12,208,208]{3,2,1,0:T(8,128)(2,1)}) custom-call(s32[2]{0:T(128)} %counts_ref.3, bf16[416,2304]{1,0:T(8,128)(2,1)} %get-tuple-element.250.query_ref.key_ref.value_ref, bf16[416,2304]{1,0:T(8,128)(2,1)} %get-tuple-element.250.query_ref.key_ref.value_ref, ...), custom_call_target="tpu_custom_call" | custom-call | tf_op jit(solution)/shard_map/attention/pallas_call | solution.py:413
  173.6 13.2 %mlp.2 = (f32[416,768]{1,0:T(8,128)}, bf16[416,768]{1,0:T(8,128)(2,1)}, f32[416,768]{1,0:T(8,128)}, bf16[416,768]{1,0:T(8,128)(2,1)}, bf16[416,3072]{1,0:T(8,128...) custom-call(bf16[416,768]{1,0:T(8,128)(2,1)} %get-tuple-element.252.attended_ref.refs_2_, ...), custom_call_target="tpu_custom_call" | custom-call | tf_op jit(solution)/shard_map/mlp/pallas_call | solution.py:672
  193.0 14.2 %project.3 = (bf16[416,768]{1,0:T(8,128)(2,1)}, bf16[416,2304]{1,0:T(8,128)(2,1)}, bf16[3456,16,128]{2,1,0:T(8,128)(2,1)}) custom-call(s32[4]{0:T(128)} %pad_add_fusion.at_ref, bf16[216,16,128]{2,1,0:T(8,128)(2,1)} %collective-permute-done.17.refs_0_, bf16[216,16,128]{2,1,0:T(8,128)(2,1)} %collective-permute-done.18.refs_1_, ...), custom_call_target="tpu_custom_call" | custom-call | tf_op jit(solution)/shard_map/project/pallas_call | solution.py:562
  207.2 7.6 %attention.3 = (bf16[416,768]{1,0:T(8,128)(2,1)}, bf16[2,12,208,208]{3,2,1,0:T(8,128)(2,1)}) custom-call(s32[2]{0:T(128)} %counts_ref.3, bf16[416,2304]{1,0:T(8,128)(2,1)} %get-tuple-element.279.query_ref.key_ref.value_ref, bf16[416,2304]{1,0:T(8,128)(2,1)} %get-tuple-element.279.query_ref.key_ref.value_ref, ...), custom_call_target="tpu_custom_call" | custom-call | tf_op jit(solution)/shard_map/attention/pallas_call | solution.py:413
  214.8 13.1 %mlp.3 = (f32[416,768]{1,0:T(8,128)}, bf16[416,768]{1,0:T(8,128)(2,1)}, f32[416,768]{1,0:T(8,128)}, bf16[416,768]{1,0:T(8,128)(2,1)}, bf16[416,3072]{1,0:T(8,128...) custom-call(bf16[416,768]{1,0:T(8,128)(2,1)} %get-tuple-element.282.attended_ref.refs_2_, ...), custom_call_target="tpu_custom_call" | custom-call | tf_op jit(solution)/shard_map/mlp/pallas_call | solution.py:672
  227.9 13.2 %mlp_back.2 = (f32[416,768]{1,0:T(8,128)}, bf16[416,768]{1,0:T(8,128)(2,1)}, bf16[416,768]{1,0:T(8,128)(2,1)}, bf16[416,3072]{1,0:T(8,128)(2,1)}, bf16[416,768]{1,0:T(8,128)(2,1)}, /*index=5*/f32[64,128]{1,0:T(8,128)}) custom-call(f32[416,768]{1,0:T(8,128)} %pad_rows.3.grad_ref, bf16[416,768]{1,0:T(8,128)(2,1)} %get-tuple-element.284.branch_ref, ...), custom_call_target="tpu_custom_call" | custom-call | tf_op jit(solution)/shard_map/mlp_back/pallas_call | solution.py:744
  241.1 10.9 %attention_back.2 = (bf16[3,416,768]{2,1,0:T(8,128)(2,1)}, f32[12,208,208]{2,1,0:T(8,128)}) custom-call(bf16[416,2304]{1,0:T(8,128)(2,1)} %get-tuple-element.279.query_ref.key_ref.value_ref, bf16[416,2304]{1,0:T(8,128)(2,1)} %get-tuple-element.279.query_ref.key_ref.value_ref, bf16[416,2304]{1,0:T(8,128)(2,1)} %get-tuple-element.279.query_ref.key_ref.value_ref, ...), custom_call_target="tpu_custom_call" | custom-call | tf_op jit(solution)/shard_map/attention_back/pallas_call | solution.py:433
  252.0 12.8 %weight_back.2 = (bf16[864,16,128]{2,1,0:T(8,128)(2,1)}, bf16[864,16,128]{2,1,0:T(8,128)(2,1)}, bf16[864,16,128]{2,1,0:T(8,128)(2,1)}, bf16[864,16,128]{2,1,0:T(8,128)(2,1)}) custom-call(s32[4]{0:T(128)} %pad_add_fusion.at_ref, bf16[416,768]{1,0:T(8,128)(2,1)} %get-tuple-element.278.refs_0_, bf16[3,416,768]{2,1,0:T(8,128)(2,1)} %get-tuple-element.290.refs_1_.project_ref, ...), custom_call_target="tpu_custom_call" | custom-call | tf_op jit(solution)/shard_map/weight_back/pallas_call | solution.py:827
  265.4 6.7 %input_back.2 = (f32[416,768]{1,0:T(8,128)}, f32[24,128]{1,0:T(8,128)}) custom-call(bf16[3,416,768]{2,1,0:T(8,128)(2,1)} %get-tuple-element.290.refs_1_.project_ref, f32[416,768]{1,0:T(8,128)} %get-tuple-element.300.grad_middle_ref, f32[416,768]{1,0:T(8,128)} %get-tuple-element.277.refs_14_.hidden_ref, f32[160,128]{1,0:T(8,128)} %get-tuple-element.452.refs_15_.vectors_ref, ...), custom_call_target="tpu_custom_call" | custom-call | tf_op jit(solution)/shard_map/input_back/pallas_call | solution.py:867
  281.4 12.8 %mlp_back.3 = (f32[416,768]{1,0:T(8,128)}, bf16[416,768]{1,0:T(8,128)(2,1)}, bf16[416,768]{1,0:T(8,128)(2,1)}, bf16[416,3072]{1,0:T(8,128)(2,1)}, bf16[416,768]{1,0:T(8,128)(2,1)}, /*index=5*/f32[64,128]{1,0:T(8,128)}) custom-call(f32[416,768]{1,0:T(8,128)} %get-tuple-element.313.grad_ref, bf16[416,768]{1,0:T(8,128)(2,1)} %get-tuple-element.314.branch_ref, ...), custom_call_target="tpu_custom_call" | custom-call | tf_op jit(solution)/shard_map/mlp_back/pallas_call | solution.py:744
  294.3 10.9 %attention_back.3 = (bf16[3,416,768]{2,1,0:T(8,128)(2,1)}, f32[12,208,208]{2,1,0:T(8,128)}) custom-call(bf16[416,2304]{1,0:T(8,128)(2,1)} %get-tuple-element.250.query_ref.key_ref.value_ref, bf16[416,2304]{1,0:T(8,128)(2,1)} %get-tuple-element.250.query_ref.key_ref.value_ref, bf16[416,2304]{1,0:T(8,128)(2,1)} %get-tuple-element.250.query_ref.key_ref.value_ref, ...), custom_call_target="tpu_custom_call" | custom-call | tf_op jit(solution)/shard_map/attention_back/pallas_call | solution.py:433
  305.1 12.9 %weight_back.3 = (bf16[864,16,128]{2,1,0:T(8,128)(2,1)}, bf16[864,16,128]{2,1,0:T(8,128)(2,1)}, bf16[864,16,128]{2,1,0:T(8,128)(2,1)}, bf16[864,16,128]{2,1,0:T(8,128)(2,1)}) custom-call(s32[4]{0:T(128)} %pad_add_fusion.at_ref, bf16[416,768]{1,0:T(8,128)(2,1)} %get-tuple-element.312.refs_0_, bf16[3,416,768]{2,1,0:T(8,128)(2,1)} %get-tuple-element.368.refs_1_.project_ref, ...), custom_call_target="tpu_custom_call" | custom-call | tf_op jit(solution)/shard_map/weight_back/pallas_call | solution.py:827
  336.9 6.6 %collective-permute-done.42 = bf16[216,16,128]{2,1,0:T(8,128)(2,1)S(1)} collective-permute-done((bf16[216,16,128]{2,1,0:T(8,128)(2,1)S(1)}, bf16[216,16,128]{2,1,0:T(8,128)(2,1)S(1)}, u32[]{:S(2)}, u32[]{:S(2)}) %collective-permute-start.42) | collective-permute-done | bytes 884768 | tf_op jit(solution)/shard_map/ppermute | solution.py:914
  351.0 15.2 %table_back.1 = f32[32,768]{1,0:T(8,128)} custom-call(f32[12,208,208]{2,1,0:T(8,128)} %get-tuple-element.374.first_ref, f32[12,208,208]{2,1,0:T(8,128)} %get-tuple-element.375.second_ref), custom_call_target="tpu_custom_call" | custom-call | tf_op jit(solution)/shard_map/table_back/pallas_call | solution.py:319
  371.4 6.6 %input_back.3 = (f32[416,768]{1,0:T(8,128)}, f32[24,128]{1,0:T(8,128)}) custom-call(bf16[3,416,768]{2,1,0:T(8,128)(2,1)} %get-tuple-element.368.refs_1_.project_ref, f32[416,768]{1,0:T(8,128)} %get-tuple-element.369.grad_middle_ref, f32[416,768]{1,0:T(8,128)} %pad_rows.2.refs_6_.hidden_ref, f32[160,128]{1,0:T(8,128)} %get-tuple-element.453.refs_7_.vectors_ref, ...), custom_call_target="tpu_custom_call" | custom-call | tf_op jit(solution)/shard_map/input_back/pallas_call | solution.py:867
  416.4 8.2 %collective-permute-start.56 = (bf16[384,128]{1,0:T(8,128)(2,1)S(1)}, bf16[384,128]{1,0:T(8,128)(2,1)S(1)}, u32[]{:S(2)}, u32[]{:S(2)}) collective-permute-start(bf16[384,128]{1,0:T(8,128)(2,1)S(1)} %bitcast.118), channel_id=1, source_target_pairs={{0,1},{1,2},{2,3},{3,4},{4,5},{5,6},{6,7},{7,8},{8,9},{9,10},{10,1... | collective-permute-start | bytes 294920 | tf_op jit(solution)/shard_map/ppermute | solution.py:116
  429.2 20.5 %collective-permute-done.57 = bf16[288,128]{1,0:T(8,128)(2,1)S(1)} collective-permute-done((bf16[288,128]{1,0:T(8,128)(2,1)S(1)}, bf16[288,128]{1,0:T(8,128)(2,1)S(1)}, u32[]{:S(2)}, u32[]{:S(2)}) %collective-permute-start.57) | collective-permute-done | bytes 73760 | tf_op jit(solution)/shard_map/ppermute | solution.py:120
  (284 shorter events, 192.4 us)
Async XLA Ops:
  18.6 32.5 %collective-permute-start.7 = (bf16[108,16,128]{2,1,0:T(8,128)(2,1)S(1)}, bf16[108,16,128]{2,1,0:T(8,128)(2,1)S(1)}, u32[]{:S(2)}, u32[]{:S(2)}) collective-permute-start(bf16[108,16,128]{2,1,0:T(8,128)(2,1)S(1)} %bitcast.112), channel_id=1, source_target_pairs={{0,4},{1,5},{2,6},{3,7},{4,0},{5,1},{6,2},{7,3},{8,12},{9,13},{10,... | collective-permute-start | bytes 1327112 | tf_op jit(solution)/shard_map/ppermute | solution.py:914
  23.4 37.1 %collective-permute-start.8 = (bf16[108,16,128]{2,1,0:T(8,128)(2,1)S(1)}, bf16[108,16,128]{2,1,0:T(8,128)(2,1)S(1)}, u32[]{:S(2)}, u32[]{:S(2)}) collective-permute-start(bf16[108,16,128]{2,1,0:T(8,128)(2,1)S(1)} %bitcast.113), channel_id=1, source_target_pairs={{0,6},{1,7},{2,4},{3,5},{4,2},{5,3},{6,0},{7,1},{8,14},{9,15},{10,... | collective-permute-start | bytes 1327112 | tf_op jit(solution)/shard_map/ppermute | solution.py:914
  35.3 25.4 %collective-permute-start.4 = (bf16[128,16,128]{2,1,0:T(8,128)(2,1)S(1)}, bf16[128,16,128]{2,1,0:T(8,128)(2,1)S(1)}, u32[]{:S(2)}, u32[]{:S(2)}) collective-permute-start(bf16[128,16,128]{2,1,0:T(8,128)(2,1)S(1)} %pad_maximum_fusion.7), channel_id=1, source_target_pairs={{0,16},{1,17},{2,18},{3,19},{4,20},{5,21},{6,22},{7,23},{8,24},{9,... | collective-permute-start | bytes 1572872 | tf_op jit(solution)/shard_map/ppermute | solution.py:914
  36.3 27.2 %collective-permute-start.9 = (bf16[108,16,128]{2,1,0:T(8,128)(2,1)S(1)}, bf16[108,16,128]{2,1,0:T(8,128)(2,1)S(1)}, u32[]{:S(2)}, u32[]{:S(2)}) collective-permute-start(bf16[108,16,128]{2,1,0:T(8,128)(2,1)S(1)} %pad_maximum_fusion.9), channel_id=1, source_target_pairs={{0,8},{1,9},{2,10},{3,11},{4,12},{5,13},{6,14},{7,15},{8,0},{9,1},... | collective-permute-start | bytes 1327112 | tf_op jit(solution)/shard_map/ppermute | solution.py:914
  66.0 25.2 %collective-permute-start.15 = (bf16[2048,128]{1,0:T(8,128)(2,1)S(1)}, bf16[2048,128]{1,0:T(8,128)(2,1)S(1)}, u32[]{:S(2)}, u32[]{:S(2)}) collective-permute-start(bf16[2048,128]{1,0:T(8,128)(2,1)S(1)} %pad_maximum_fusion.8), channel_id=1, source_target_pairs={{0,4},{1,5},{2,6},{3,7},{4,0},{5,1},{6,2},{7,3},{8,12},{9,13},{10,... | collective-permute-start | bytes 1572872 | tf_op jit(solution)/shard_map/ppermute | solution.py:914
  68.4 45.1 %collective-permute-start.16 = (bf16[2048,128]{1,0:T(8,128)(2,1)S(1)}, bf16[2048,128]{1,0:T(8,128)(2,1)S(1)}, u32[]{:S(2)}, u32[]{:S(2)}) collective-permute-start(bf16[2048,128]{1,0:T(8,128)(2,1)S(1)} %pad_maximum_fusion.8), channel_id=1, source_target_pairs={{0,6},{1,7},{2,4},{3,5},{4,2},{5,3},{6,0},{7,1},{8,14},{9,15},{10,... | collective-permute-start | bytes 1572872 | tf_op jit(solution)/shard_map/ppermute | solution.py:914
  80.3 36.2 %collective-permute-start.13 = (bf16[324,16,128]{2,1,0:T(8,128)(2,1)S(1)}, bf16[324,16,128]{2,1,0:T(8,128)(2,1)S(1)}, u32[]{:S(2)}, u32[]{:S(2)}) collective-permute-start(bf16[324,16,128]{2,1,0:T(8,128)(2,1)S(1)} %pad_maximum_fusion.1), channel_id=1, source_target_pairs={{0,8},{1,9},{2,10},{3,11},{4,12},{5,13},{6,14},{7,15},{8,0},{9,1},... | collective-permute-start | bytes 3981320 | tf_op jit(solution)/shard_map/ppermute | solution.py:914
  81.6 34.9 %collective-permute-start.11 = (bf16[324,16,128]{2,1,0:T(8,128)(2,1)S(1)}, bf16[324,16,128]{2,1,0:T(8,128)(2,1)}, u32[]{:S(2)}, u32[]{:S(2)}) collective-permute-start(bf16[324,16,128]{2,1,0:T(8,128)(2,1)S(1)} %pad_maximum_fusion), channel_id=1, source_target_pairs={{0,16},{1,17},{2,18},{3,19},{4,20},{5,21},{6,22},{7,23},{8,24},{9,... | collective-permute-start | bytes 3981320 | tf_op jit(solution)/shard_map/ppermute | solution.py:914
  119.4 42.7 %collective-permute-start.17 = (bf16[216,16,128]{2,1,0:T(8,128)(2,1)S(1)}, bf16[216,16,128]{2,1,0:T(8,128)(2,1)}, u32[]{:S(2)}, u32[]{:S(2)}) collective-permute-start(bf16[216,16,128]{2,1,0:T(8,128)(2,1)S(1)} %pad_maximum_fusion.3), channel_id=1, source_target_pairs={{0,8},{1,9},{2,10},{3,11},{4,12},{5,13},{6,14},{7,15},{8,0},{9,1},... | collective-permute-start | bytes 2654216 | tf_op jit(solution)/shard_map/ppermute | solution.py:914
  120.3 41.8 %collective-permute-start.18 = (bf16[216,16,128]{2,1,0:T(8,128)(2,1)S(1)}, bf16[216,16,128]{2,1,0:T(8,128)(2,1)}, u32[]{:S(2)}, u32[]{:S(2)}) collective-permute-start(bf16[216,16,128]{2,1,0:T(8,128)(2,1)S(1)} %pad_maximum_fusion.4), channel_id=1, source_target_pairs={{0,16},{1,17},{2,18},{3,19},{4,20},{5,21},{6,22},{7,23},{8,24},{9,... | collective-permute-start | bytes 2654216 | tf_op jit(solution)/shard_map/ppermute | solution.py:914
  129.5 32.6 %collective-permute-start.22 = (bf16[216,16,128]{2,1,0:T(8,128)(2,1)S(1)}, bf16[216,16,128]{2,1,0:T(8,128)(2,1)}, u32[]{:S(2)}, u32[]{:S(2)}) collective-permute-start(bf16[216,16,128]{2,1,0:T(8,128)(2,1)S(1)} %pad_maximum_fusion.3), channel_id=1, source_target_pairs={{0,16},{1,17},{2,18},{3,19},{4,20},{5,21},{6,22},{7,23},{8,24},{9,... | collective-permute-start | bytes 2654216 | tf_op jit(solution)/shard_map/ppermute | solution.py:914
  130.5 31.6 %collective-permute-start.23 = (bf16[216,16,128]{2,1,0:T(8,128)(2,1)S(1)}, bf16[216,16,128]{2,1,0:T(8,128)(2,1)}, u32[]{:S(2)}, u32[]{:S(2)}) collective-permute-start(bf16[216,16,128]{2,1,0:T(8,128)(2,1)S(1)} %pad_maximum_fusion.4), channel_id=1, source_target_pairs={{0,8},{1,9},{2,10},{3,11},{4,12},{5,13},{6,14},{7,15},{8,0},{9,1},... | collective-permute-start | bytes 2654216 | tf_op jit(solution)/shard_map/ppermute | solution.py:914
  135.0 51.9 %collective-permute-start.30 = (bf16[432,16,128]{2,1,0:T(8,128)(2,1)S(1)}, bf16[432,16,128]{2,1,0:T(8,128)(2,1)S(1)}, u32[]{:S(2)}, u32[]{:S(2)}) collective-permute-start(bf16[432,16,128]{2,1,0:T(8,128)(2,1)S(1)} %constant_dynamic-update-slice_fusion.10.refs_8_), channel_id=1, source_target_pairs={{0,1},{1,0},{2,3},{3,2},{4,5},{5,4},{6,7},{7,6},{8,9},{9,8},{10,11... | collective-permute-start | bytes 5308424 | tf_op jit(solution)/shard_map/ppermute | solution.py:914
  280.6 40.0 %collective-permute-start.36 = (bf16[432,16,128]{2,1,0:T(8,128)(2,1)}, bf16[432,16,128]{2,1,0:T(8,128)(2,1)S(1)}, u32[]{:S(2)}, u32[]{:S(2)}) collective-permute-start(bf16[432,16,128]{2,1,0:T(8,128)(2,1)} %get-tuple-element.311), channel_id=1, source_target_pairs={{0,16},{1,17},{2,18},{3,19},{4,20},{5,21},{6,22},{7,23},{8,24},{9,... | collective-permute-start | bytes 5308424 | tf_op jit(solution)/shard_map/ppermute | solution.py:914
  280.9 39.7 %collective-permute-start.35 = (bf16[432,16,128]{2,1,0:T(8,128)(2,1)}, bf16[432,16,128]{2,1,0:T(8,128)(2,1)S(1)}, u32[]{:S(2)}, u32[]{:S(2)}) collective-permute-start(bf16[432,16,128]{2,1,0:T(8,128)(2,1)} %get-tuple-element.306), channel_id=1, source_target_pairs={{0,8},{1,9},{2,10},{3,11},{4,12},{5,13},{6,14},{7,15},{8,0},{9,1},... | collective-permute-start | bytes 5308424 | tf_op jit(solution)/shard_map/ppermute | solution.py:914
  335.4 46.7 %collective-permute-start.40 = (bf16[432,16,128]{2,1,0:T(8,128)(2,1)}, bf16[432,16,128]{2,1,0:T(8,128)(2,1)}, u32[]{:S(2)}, u32[]{:S(2)}) collective-permute-start(bf16[432,16,128]{2,1,0:T(8,128)(2,1)} %get-tuple-element.355), channel_id=1, source_target_pairs={{0,16},{1,17},{2,18},{3,19},{4,20},{5,21},{6,22},{7,23},{8,24},{9,... | collective-permute-start | bytes 5308424 | tf_op jit(solution)/shard_map/ppermute | solution.py:914
  336.6 45.6 %collective-permute-start.39 = (bf16[432,16,128]{2,1,0:T(8,128)(2,1)}, bf16[432,16,128]{2,1,0:T(8,128)(2,1)}, u32[]{:S(2)}, u32[]{:S(2)}) collective-permute-start(bf16[432,16,128]{2,1,0:T(8,128)(2,1)} %get-tuple-element.347), channel_id=1, source_target_pairs={{0,8},{1,9},{2,10},{3,11},{4,12},{5,13},{6,14},{7,15},{8,0},{9,1},... | collective-permute-start | bytes 5308424 | tf_op jit(solution)/shard_map/ppermute | solution.py:914
  346.8 32.1 %collective-permute-start.45 = (bf16[108,16,128]{2,1,0:T(8,128)(2,1)}, bf16[108,16,128]{2,1,0:T(8,128)(2,1)}, u32[]{:S(2)}, u32[]{:S(2)}) collective-permute-start(bf16[108,16,128]{2,1,0:T(8,128)(2,1)} %pad_maximum_fusion.13), channel_id=1, source_target_pairs={{0,6},{1,7},{2,4},{3,5},{4,2},{5,3},{6,0},{7,1},{8,14},{9,15},{10,... | collective-permute-start | bytes 1327112 | tf_op jit(solution)/shard_map/ppermute | solution.py:914
  348.8 30.1 %collective-permute-start.44 = (bf16[108,16,128]{2,1,0:T(8,128)(2,1)}, bf16[108,16,128]{2,1,0:T(8,128)(2,1)}, u32[]{:S(2)}, u32[]{:S(2)}) collective-permute-start(bf16[108,16,128]{2,1,0:T(8,128)(2,1)} %pad_maximum_fusion.12), channel_id=1, source_target_pairs={{0,4},{1,5},{2,6},{3,7},{4,0},{5,1},{6,2},{7,3},{8,12},{9,13},{10,... | collective-permute-start | bytes 1327112 | tf_op jit(solution)/shard_map/ppermute | solution.py:914
  349.6 29.3 %collective-permute-start.43 = (bf16[108,16,128]{2,1,0:T(8,128)(2,1)}, bf16[108,16,128]{2,1,0:T(8,128)(2,1)}, u32[]{:S(2)}, u32[]{:S(2)}) collective-permute-start(bf16[108,16,128]{2,1,0:T(8,128)(2,1)} %pad_maximum_fusion.11), channel_id=1, source_target_pairs={{0,2},{1,3},{2,0},{3,1},{4,6},{5,7},{6,4},{7,5},{8,10},{9,11},{10,... | collective-permute-start | bytes 1327112 | tf_op jit(solution)/shard_map/ppermute | solution.py:914
  407.4 46.0 %collective-permute-start.53 = (bf16[108,16,128]{2,1,0:T(8,128)(2,1)S(1)}, bf16[108,16,128]{2,1,0:T(8,128)(2,1)S(1)}, u32[]{:S(2)}, u32[]{:S(2)}) collective-permute-start(bf16[108,16,128]{2,1,0:T(8,128)(2,1)S(1)} %pad_maximum_fusion.17), channel_id=1, source_target_pairs={{0,6},{1,7},{2,4},{3,5},{4,2},{5,3},{6,0},{7,1},{8,14},{9,15},{10,... | collective-permute-start | bytes 1327112 | tf_op jit(solution)/shard_map/ppermute | solution.py:914
  408.7 44.7 %collective-permute-start.52 = (bf16[108,16,128]{2,1,0:T(8,128)(2,1)S(1)}, bf16[108,16,128]{2,1,0:T(8,128)(2,1)S(1)}, u32[]{:S(2)}, u32[]{:S(2)}) collective-permute-start(bf16[108,16,128]{2,1,0:T(8,128)(2,1)S(1)} %pad_maximum_fusion.16), channel_id=1, source_target_pairs={{0,4},{1,5},{2,6},{3,7},{4,0},{5,1},{6,2},{7,3},{8,12},{9,13},{10,... | collective-permute-start | bytes 1327112 | tf_op jit(solution)/shard_map/ppermute | solution.py:914
  411.8 41.6 %collective-permute-start.51 = (bf16[108,16,128]{2,1,0:T(8,128)(2,1)S(1)}, bf16[108,16,128]{2,1,0:T(8,128)(2,1)S(1)}, u32[]{:S(2)}, u32[]{:S(2)}) collective-permute-start(bf16[108,16,128]{2,1,0:T(8,128)(2,1)S(1)} %pad_maximum_fusion.15), channel_id=1, source_target_pairs={{0,2},{1,3},{2,0},{3,1},{4,6},{5,7},{6,4},{7,5},{8,10},{9,11},{10,... | collective-permute-start | bytes 1327112 | tf_op jit(solution)/shard_map/ppermute | solution.py:914
  416.4 33.2 %collective-permute-start.56 = (bf16[384,128]{1,0:T(8,128)(2,1)S(1)}, bf16[384,128]{1,0:T(8,128)(2,1)S(1)}, u32[]{:S(2)}, u32[]{:S(2)}) collective-permute-start(bf16[384,128]{1,0:T(8,128)(2,1)S(1)} %bitcast.118), channel_id=1, source_target_pairs={{0,1},{1,2},{2,3},{3,4},{4,5},{5,6},{6,7},{7,8},{8,9},{9,10},{10,1... | collective-permute-start | bytes 294920 | tf_op jit(solution)/shard_map/ppermute | solution.py:116
  (61 other events, 617.3 us)
